TPU v7x, 512 devices: a whole 4x4x16 slice. The times are simulated.
512 devices in a mesh: wide: 128 (over z, x, core), narrow: 4 (over y).
Axes of the slice: x: 4, y: 4, z: 16, core: 2. Of those that a mesh axis runs over, the one named last changes fastest.
Arguments:
- queries: bfloat16 [262144, 1024], P(('wide', 'narrow')), may hold values from -0.25 to 0.25
- responses: bfloat16 [262144, 1024], P(('wide', 'narrow')), may hold values from -0.25 to 0.25
- block_cluster: int32 [2048], replicated, may hold values from 0 to 2047, as said below
Outputs:
- query_loss: float32 [262144], P(('wide', 'narrow'))
- response_loss: float32 [262144], P(('wide', 'narrow'))
- query_grad: bfloat16 [262144, 1024], P(('wide', 'narrow'))
- response_grad: bfloat16 [262144, 1024], P(('wide', 'narrow'))
Inputs may be any that keep to these rules, and one draw needn't show every extreme that they name: block_cluster[b] is the first block of b's cluster, so it never falls and is at most b; every aligned group of 4 blocks has a cluster start after its first block, and the first block of every group but the first continues the cluster of the block before it.
All inputs are finite; a program needn't handle non-finite values.
Results may differ from a plain program's by a relative error of at most 0.0065.
Values may be sent and summed in bfloat16 or wider, within the bound.
A program may use at most 64 MiB of HBM per device.

v0:
```python
import jax
import jax.numpy as jnp
from jax import lax
from jax.sharding import PartitionSpec as P

BLK = 128


logit_scale = 20.0
masked_value = -1e30


def shifted_2(shard, axis, by):
    devices = lax.axis_size(axis)
    pairs = [(i, i + by) for i in range(devices) if 0 <= i + by < devices]
    return lax.ppermute(shard, axis, pairs)


def dot_rows(former, latter):
    return lax.dot_general(
        former, latter, (((1,), (1,)), ((), ())), preferred_element_type=jnp.float32
    )


def dot_cols(former, latter):
    return lax.dot_general(
        former, latter, (((0,), (0,)), ((), ())), preferred_element_type=jnp.float32
    )


def masked_stats(scores, allowed, reduce_dim):
    largest = jnp.max(jnp.where(allowed, scores, masked_value), axis=reduce_dim)
    shifted = scores - jnp.expand_dims(largest, reduce_dim)
    summed = jnp.sum(jnp.exp(jnp.where(allowed, shifted, masked_value)), axis=reduce_dim)
    return (largest, summed)


def combine(former, latter):
    largest = jnp.maximum(former[0], latter[0])
    summed = former[1] * jnp.exp(former[0] - largest) + latter[1] * jnp.exp(latter[0] - largest)
    return (largest, summed)


def finish(stats):
    return stats[0] + jnp.log(stats[1])


def pad_front(values, count, filler):
    front = jnp.full((count,) + values.shape[1:], filler, values.dtype)
    return jnp.concatenate([front, values], 0)


def pair_weights(scores, allowed, lse_for_rows, lse_for_cols):
    return jnp.where(
        allowed,
        jnp.exp(scores - lse_for_rows[:, None]) + jnp.exp(scores - lse_for_cols[None, :]),
        0.0,
    )


def shards(queries, responses, block_cluster):
    row_count = queries.shape[0]
    block_count = row_count // BLK
    skipped = 0
    kept = row_count - skipped
    position = lax.axis_index(("wide", "narrow"))
    own_blocks = lax.dynamic_slice_in_dim(block_cluster, position * block_count, block_count)
    left_blocks = lax.dynamic_slice_in_dim(
        block_cluster, jnp.maximum(position - 1, 0) * block_count, block_count
    )
    left_blocks = jnp.where(position > 0, left_blocks, -1)
    own_ids = jnp.repeat(own_blocks, BLK, total_repeat_length=row_count)
    left_ids = jnp.repeat(left_blocks, BLK, total_repeat_length=row_count)[skipped:]
    left_queries, left_responses = shifted_2((queries, responses), ("wide", "narrow"), 1)
    window_responses = jnp.concatenate([left_responses, responses], 0)
    window_ids = jnp.concatenate([left_ids, own_ids], 0)
    scores_own = dot_rows(queries, window_responses) * logit_scale
    mask_own = own_ids[:, None] == window_ids[None, :]
    scores_left = dot_rows(left_queries, responses) * logit_scale
    mask_left = left_ids[:, None] == own_ids[None, :]
    row_own = masked_stats(scores_own, mask_own, 1)
    col_window = masked_stats(scores_own, mask_own, 0)
    col_left = (col_window[0][:kept], col_window[1][:kept])
    row_left = masked_stats(scores_left, mask_left, 1)
    col_own = combine(
        (col_window[0][kept:], col_window[1][kept:]), masked_stats(scores_left, mask_left, 0)
    )
    from_right = shifted_2(
        (row_left[0], row_left[1], col_left[0], col_left[1]), ("wide", "narrow"), -1
    )
    right_rows = (
        pad_front(from_right[0], skipped, masked_value),
        pad_front(from_right[1], skipped, 0.0),
    )
    right_cols = (
        pad_front(from_right[2], skipped, masked_value),
        pad_front(from_right[3], skipped, 0.0),
    )
    lse_rows = finish(combine(row_own, right_rows))
    lse_cols = finish(combine(col_own, right_cols))
    lse_left_rows, lse_left_cols = shifted_2(
        (lse_rows[skipped:], lse_cols[skipped:]), ("wide", "narrow"), 1
    )
    diagonal = jnp.diagonal(scores_own[:, kept:])
    query_loss = lse_rows - diagonal
    response_loss = lse_cols - diagonal
    lse_window = jnp.concatenate([lse_left_cols, lse_cols], 0)
    identity_part = (
        jnp.arange(kept + row_count)[None, :] == jnp.arange(row_count)[:, None] + kept
    ).astype(jnp.float32)
    grad_own = (
        pair_weights(scores_own, mask_own, lse_rows, lse_window) - 2.0 * identity_part
    ).astype(jnp.bfloat16)
    grad_left = pair_weights(scores_left, mask_left, lse_left_rows, lse_cols).astype(jnp.bfloat16)
    query_sum = jnp.dot(grad_own, window_responses, preferred_element_type=jnp.float32)
    response_window = dot_cols(grad_own, queries)
    response_sum = response_window[kept:] + dot_cols(grad_left, left_queries)
    query_term = jnp.dot(grad_left, responses, preferred_element_type=jnp.float32)
    got_queries, got_responses = (
        shifted_2(query_term.astype(jnp.bfloat16), ("wide", "narrow"), -1).astype(query_term.dtype),
        shifted_2(response_window[:kept].astype(jnp.bfloat16), ("wide", "narrow"), -1).astype(
            jnp.float32
        ),
    )
    query_sum = query_sum + pad_front(got_queries, skipped, 0.0)
    response_sum = response_sum + pad_front(got_responses, skipped, 0.0)
    query_grad = (query_sum * logit_scale).astype(jnp.bfloat16)
    response_grad = (response_sum * logit_scale).astype(jnp.bfloat16)
    return (query_loss, response_loss, query_grad, response_grad)


def solution(mesh):
    placed = (P(("wide", "narrow"), None), P(("wide", "narrow"), None), P())
    return jax.shard_map(
        shards,
        mesh=mesh,
        in_specs=placed,
        out_specs=(
            P(("wide", "narrow")),
            P(("wide", "narrow")),
            P(("wide", "narrow"), None),
            P(("wide", "narrow"), None),
        ),
        check_vma=False,
    )
```

profile of v0, /device:TPU:481, one launch (start us, length us, event | category | flops | bytes accessed | tf_op | source)
XLA Modules:
  0.0 125.6 jit_solution(6438724706633760088)
XLA Ops:
  0.6 3.2 %collective-permute-start.1 = (bf16[512,1024]{1,0:T(8,128)(2,1)}, bf16[512,1024]{1,0:T(8,128)(2,1)S(1)}, u32[]{:S(2)}, u32[]{:S(2)}) collective-permute-start(bf16[512,1024]{1,0:T(8,128)(2,1)} %param.9), channel_id=1, source_target_pairs={{0,1},{1,2},{2,3},{3,4},{4,5},{5,6},{6,7},{7,8},{8,9},{9,10},{10,1... | collective-permute-start | bytes 3145736 | tf_op jit(solution)/shard_map/ppermute | solution.py:16
  3.8 3.2 %collective-permute-start = (bf16[512,1024]{1,0:T(8,128)(2,1)}, bf16[512,1024]{1,0:T(8,128)(2,1)S(1)}, u32[]{:S(2)}, u32[]{:S(2)}) collective-permute-start(bf16[512,1024]{1,0:T(8,128)(2,1)} %param.10), channel_id=1, source_target_pairs={{0,1},{1,2},{2,3},{3,4},{4,5},{5,6},{6,7},{7,8},{8,9},{9,10},{10,1... | collective-permute-start | bytes 3145736 | tf_op jit(solution)/shard_map/ppermute | solution.py:16
  7.1 0.8 broadcast_select_fusion
  7.9 0.6 fusion.34
  8.5 2.6 %select_select_fusion = s32[512]{0:T(512)S(1)} fusion(s32[]{:T(128)} %bitcast.8, s32[]{:T(128)} %bitcast.7, s32[]{:T(128)} %bitcast.6, s32[]{:T(128)} %bitcast.5), kind=kLoop, calls=%fused_computation.39 | loop fusion | flops 7680 | bytes 2064 | tf_op jit(solution)/shard_map/jit(_take)/select_n | solution.py:73
  11.1 2.4 %select_select_fusion.1 = s32[512]{0:T(512)S(1)} fusion(s32[]{:T(128)} %bitcast.4, s32[]{:T(128)} %bitcast.3, s32[]{:T(128)} %bitcast.2, s32[]{:T(128)} %bitcast.1), kind=kLoop, calls=%fused_computation.40 | loop fusion | flops 7680 | bytes 2064 | tf_op jit(solution)/shard_map/jit(_take)/select_n | solution.py:72
  13.6 27.4 %collective-permute-done.1 = bf16[512,1024]{1,0:T(8,128)(2,1)S(1)} collective-permute-done((bf16[512,1024]{1,0:T(8,128)(2,1)}, bf16[512,1024]{1,0:T(8,128)(2,1)S(1)}, u32[]{:S(2)}, u32[]{:S(2)}) %collective-permute-start.1) | collective-permute-done | bytes 1048608 | tf_op jit(solution)/shard_map/ppermute | solution.py:16
  41.0 0.0 copy-start.7
  41.0 2.5 %fusion.16 = (f32[512]{0:T(512)S(1)}, f32[512]{0:T(512)S(1)}, f32[512,512]{1,0:T(8,128)S(1)}) fusion(s32[512]{0:T(512)S(1)} %select_select_fusion.1, s32[512]{0:T(512)S(1)} %select_select_fusion, bf16[512,1024]{1,0:T(8,128)(2,1)S(1)} %collective-permute-done.1, bf16[512,1024]{1,0:T(8,128)(2,1)} %param.10), kind=kOutput, calls=%fused_computation.32 | convolution fusion | flops 538180608 | bytes 3153920 | tf_op jit(solution)/shard_map/dot_general | solution.py:20
  43.4 0.0 copy-done.7
  43.5 0.0 copy-start.1
  43.5 0.0 copy-start
  43.5 2.1 %collective-permute-start.2 = (f32[512]{0:T(512)S(1)}, f32[512]{0:T(512)S(1)}, u32[]{:S(2)}, u32[]{:S(2)}) collective-permute-start(f32[512]{0:T(512)S(1)} %get-tuple-element.32), channel_id=1, source_target_pairs={{1,0},{2,1},{3,2},{4,3},{5,4},{6,5},{7,6},{8,7},{9,8},{10,9},{11,1... | collective-permute-start | bytes 6152 | tf_op jit(solution)/shard_map/ppermute | solution.py:16
  45.5 0.5 fusion.14
  46.1 0.0 copy-start.5
  46.1 2.1 %collective-permute-start.3 = (f32[512]{0:T(512)S(1)}, f32[512]{0:T(512)S(1)}, u32[]{:S(2)}, u32[]{:S(2)}) collective-permute-start(f32[512]{0:T(512)S(1)} %get-tuple-element.30), channel_id=1, source_target_pairs={{1,0},{2,1},{3,2},{4,3},{5,4},{6,5},{7,6},{8,7},{9,8},{10,9},{11,1... | collective-permute-start | bytes 6152 | tf_op jit(solution)/shard_map/ppermute | solution.py:16
  48.1 4.1 %collective-permute-done = bf16[512,1024]{1,0:T(8,128)(2,1)S(1)} collective-permute-done((bf16[512,1024]{1,0:T(8,128)(2,1)}, bf16[512,1024]{1,0:T(8,128)(2,1)S(1)}, u32[]{:S(2)}, u32[]{:S(2)}) %collective-permute-start) | collective-permute-done | bytes 1048608 | tf_op jit(solution)/shard_map/ppermute | solution.py:16
  52.2 0.1 constant_dynamic-update-slice_fusion.1
  52.3 0.0 copy-done.1
  52.3 0.0 copy-done
  52.3 0.1 constant_dynamic-update-slice_fusion
  52.4 0.0 copy-done.5
  52.4 0.0 copy-start.3
  52.4 1.4 %fusion.9 = (f32[1024]{0:T(1024)S(1)}, f32[512]{0:T(512)S(1)}, f32[512,1024]{0,1:T(8,128)S(1)}) fusion(s32[512]{0:T(512)S(1)} %select_select_fusion.1, s32[1024]{0:T(1024)S(1)} %pad_add_fusion, bf16[1024,1024]{1,0:T(8,128)(2,1)S(1)} %constant_dynamic-update-slice_fusion, bf16[512,1024]{1,0:T(8,128)(2,1)S(1)} %copy-done.5), kind=kOutput, calls=%fused_computation.23 | convolution fusion | flops 1076361728 | bytes 5255168 | tf_op jit(solution)/shard_map/dot_general | solution.py:20
  53.9 0.0 copy-done.3
  53.9 1.2 fusion.3
  55.1 3.1 %collective-permute-start.5 = (f32[512]{0:T(512)S(1)}, f32[512]{0:T(512)S(1)}, u32[]{:S(2)}, u32[]{:S(2)}) collective-permute-start(f32[512]{0:T(512)S(1)} %slice.49), channel_id=1, source_target_pairs={{1,0},{2,1},{3,2},{4,3},{5,4},{6,5},{7,6},{8,7},{9,8},{10,9},{11,1... | collective-permute-start | bytes 6152 | tf_op jit(solution)/shard_map/ppermute | solution.py:16
  58.2 2.7 %collective-permute-start.4 = (f32[512]{0:T(512)S(1)}, f32[512]{0:T(512)S(1)}, u32[]{:S(2)}, u32[]{:S(2)}) collective-permute-start(f32[512]{0:T(512)S(1)} %slice.47), channel_id=1, source_target_pairs={{1,0},{2,1},{3,2},{4,3},{5,4},{6,5},{7,6},{8,7},{9,8},{10,9},{11,1... | collective-permute-start | bytes 6152 | tf_op jit(solution)/shard_map/ppermute | solution.py:16
  60.8 0.1 slice.72
  60.9 4.5 %gather_fusion = f32[512]{0:T(512)S(1)} fusion(f32[512,512]{0,1:T(8,128)S(1)} %slice.72, s32[512]{0:T(512)S(1)} %bitcast.45), kind=kCustom, calls=%fused_computation | custom fusion | bytes 8192 | tf_op jit(solution)/shard_map/jit(diagonal)/cond/branch_0_fun/gather | solution.py:104
  65.5 0.0 collective-permute-done.3
  65.5 0.0 collective-permute-done.2
  65.5 0.0 collective-permute-done.5
  65.5 0.0 collective-permute-done.4
  65.5 0.6 fusion.32
  66.1 2.6 %collective-permute-start.7 = (f32[512]{0:T(512)S(1)}, f32[512]{0:T(512)S(1)}, u32[]{:S(2)}, u32[]{:S(2)}) collective-permute-start(f32[512]{0:T(512)S(1)} %get-tuple-element.40), channel_id=1, source_target_pairs={{0,1},{1,2},{2,3},{3,4},{4,5},{5,6},{6,7},{7,8},{8,9},{9,10},{10,1... | collective-permute-start | bytes 6152 | tf_op jit(solution)/shard_map/ppermute | solution.py:16
  68.8 0.0 copy-start.6
  68.8 2.3 %collective-permute-start.6 = (f32[512]{0:T(512)S(1)}, f32[512]{0:T(512)S(1)}, u32[]{:S(2)}, u32[]{:S(2)}) collective-permute-start(f32[512]{0:T(512)S(1)} %get-tuple-element.34), channel_id=1, source_target_pairs={{0,1},{1,2},{2,3},{3,4},{4,5},{5,6},{6,7},{7,8},{8,9},{9,10},{10,1... | collective-permute-start | bytes 6152 | tf_op jit(solution)/shard_map/ppermute | solution.py:16
  71.1 1.1 collective-permute-done.7
  72.2 2.4 %convolution_convert_fusion = bf16[512,1024]{1,0:T(8,128)(2,1)S(1)} fusion(bf16[512,1024]{1,0:T(8,128)(2,1)} %param.10, f32[512,512]{1,0:T(8,128)} %copy-done.1, f32[512]{0:T(512)S(1)} %get-tuple-element.34, f32[512]{0:T(512)S(1)} %collective-permute-done.7, s32[512]{0:T(512)S(1)} %select_select_fusion.1, s32[512]{0:T(512)S(1)} %select_select_fusion), kind=kOutput, calls=%fused_computation.25 | convolution fusion | flops 538968064 | bytes 3153920 | tf_op jit(solution)/shard_map/dot_general | solution.py:118
  74.6 3.5 %collective-permute-start.8 = (bf16[512,1024]{1,0:T(8,128)(2,1)S(1)}, bf16[512,1024]{1,0:T(8,128)(2,1)S(1)}, u32[]{:S(2)}, u32[]{:S(2)}) collective-permute-start(bf16[512,1024]{1,0:T(8,128)(2,1)S(1)} %convolution_convert_fusion), channel_id=1, source_target_pairs={{1,0},{2,1},{3,2},{4,3},{5,4},{6,5},{7,6},{8,7},{9,8},{10,9},{11,1... | collective-permute-start | bytes 3145736 | tf_op jit(solution)/shard_map/ppermute | solution.py:16
  78.1 0.0 collective-permute-done.6
  78.1 0.0 copy-done.6
  78.2 1.8 %fusion.29 = f32[1024,1024]{1,0:T(8,128)S(1)} fusion(bf16[512,1024]{1,0:T(8,128)(2,1)S(1)} %copy-done.6, f32[512,1024]{0,1:T(8,128)S(1)} %get-tuple-element.49, s32[512]{0:T(512)S(1)} %iota_add_fusion, f32[1024]{0:T(1024)S(1)} %pad_maximum_fusion, f32[512]{0:T(512)S(1)} %get-tuple-element.40, s32[512]{0:T(512)S(1)} %select_select_fusion.1, ...), kind=kOutput, calls=%fused_computation.59 | convolution fusion | flops 1078460416 | bytes 7354368 | tf_op jit(solution)/shard_map/dot_general | solution.py:26
  80.0 0.0 copy-start.4
  80.0 0.2 slice.85
  80.1 0.0 copy-start.2
  80.2 0.0 copy-start.8
  80.2 3.5 %collective-permute-start.9 = (bf16[512,1024]{1,0:T(8,128)(2,1)S(1)}, bf16[512,1024]{1,0:T(8,128)(2,1)S(1)}, u32[]{:S(2)}, u32[]{:S(2)}) collective-permute-start(bf16[512,1024]{1,0:T(8,128)(2,1)S(1)} %slice.85), channel_id=1, source_target_pairs={{1,0},{2,1},{3,2},{4,3},{5,4},{6,5},{7,6},{8,7},{9,8},{10,9},{11,1... | collective-permute-start | bytes 3145736 | tf_op jit(solution)/shard_map/ppermute | solution.py:16
  83.7 28.6 %collective-permute-done.8 = bf16[512,1024]{1,0:T(8,128)(2,1)S(1)} collective-permute-done((bf16[512,1024]{1,0:T(8,128)(2,1)S(1)}, bf16[512,1024]{1,0:T(8,128)(2,1)S(1)}, u32[]{:S(2)}, u32[]{:S(2)}) %collective-permute-start.8) | collective-permute-done | bytes 1048608 | tf_op jit(solution)/shard_map/ppermute | solution.py:16
  112.3 0.0 copy-done.4
  112.3 2.7 %multiply_convert_fusion = bf16[512,1024]{1,0:T(8,128)(2,1)} fusion(bf16[512,1024]{1,0:T(8,128)(2,1)S(1)} %collective-permute-done.8, bf16[1024,1024]{1,0:T(8,128)(2,1)S(1)} %copy-done.4, f32[512,1024]{0,1:T(8,128)S(1)} %get-tuple-element.49, s32[512]{0:T(512)S(1)} %iota_add_fusion, f32[1024]{0:T(1024)S(1)} %pad_maximum_fusion, ...), kind=kOutput, calls=%fused_computation.16 | convolution fusion | flops 1080557568 | bytes 6305792 | tf_op jit(solution)/shard_map/dot_general | solution.py:115
  115.0 8.5 %collective-permute-done.9 = bf16[512,1024]{1,0:T(8,128)(2,1)S(1)} collective-permute-done((bf16[512,1024]{1,0:T(8,128)(2,1)S(1)}, bf16[512,1024]{1,0:T(8,128)(2,1)S(1)}, u32[]{:S(2)}, u32[]{:S(2)}) %collective-permute-start.9) | collective-permute-done | bytes 1048608 | tf_op jit(solution)/shard_map/ppermute | solution.py:16
  123.5 0.0 copy-done.2
  123.5 0.0 copy-done.8
  123.5 2.0 %fusion.8 = bf16[512,1024]{1,0:T(8,128)(2,1)} fusion(f32[1024,1024]{1,0:T(8,128)S(1)} %fusion.29, bf16[512,1024]{1,0:T(8,128)(2,1)S(1)} %collective-permute-done.9, bf16[512,1024]{1,0:T(8,128)(2,1)S(1)} %copy-done.8, f32[512,512]{1,0:T(8,128)S(1)} %copy-done.2, f32[512]{0:T(512)S(1)} %get-tuple-element.34, f32[512]{0:T(512)S(1)} %collective-permute-done.7, ...), kind=kOutput, calls=%fused_computation.15 | convolution fusion | flops 541065216 | bytes 6299648 | tf_op jit(solution)/shard_map/dot_general | solution.py:26
  (6 shorter events, 0.0 us)
Async XLA Ops:
  0.6 40.4 %collective-permute-start.1 = (bf16[512,1024]{1,0:T(8,128)(2,1)}, bf16[512,1024]{1,0:T(8,128)(2,1)S(1)}, u32[]{:S(2)}, u32[]{:S(2)}) collective-permute-start(bf16[512,1024]{1,0:T(8,128)(2,1)} %param.9), channel_id=1, source_target_pairs={{0,1},{1,2},{2,3},{3,4},{4,5},{5,6},{6,7},{7,8},{8,9},{9,10},{10,1... | collective-permute-start | bytes 3145736 | tf_op jit(solution)/shard_map/ppermute | solution.py:16
  3.8 48.4 %collective-permute-start = (bf16[512,1024]{1,0:T(8,128)(2,1)}, bf16[512,1024]{1,0:T(8,128)(2,1)S(1)}, u32[]{:S(2)}, u32[]{:S(2)}) collective-permute-start(bf16[512,1024]{1,0:T(8,128)(2,1)} %param.10), channel_id=1, source_target_pairs={{0,1},{1,2},{2,3},{3,4},{4,5},{5,6},{6,7},{7,8},{8,9},{9,10},{10,1... | collective-permute-start | bytes 3145736 | tf_op jit(solution)/shard_map/ppermute | solution.py:16
  41.0 2.5 %copy-start.7 = (bf16[512,1024]{1,0:T(8,128)(2,1)}, bf16[512,1024]{1,0:T(8,128)(2,1)S(1)}, u32[]{:S(2)}) copy-start(bf16[512,1024]{1,0:T(8,128)(2,1)S(1)} %collective-permute-done.1) | copy-start | bytes 3145732
  43.5 8.8 %copy-start.1 = (f32[512,512]{1,0:T(8,128)}, f32[512,512]{1,0:T(8,128)S(1)}, u32[]{:S(2)}) copy-start(f32[512,512]{1,0:T(8,128)S(1)} %get-tuple-element.50) | copy-start | bytes 3145732
  43.5 8.8 %copy-start = (bf16[512,1024]{1,0:T(8,128)(2,1)S(1)}, bf16[512,1024]{1,0:T(8,128)(2,1)}, u32[]{:S(2)}) copy-start(bf16[512,1024]{1,0:T(8,128)(2,1)} %param.10) | copy-start | bytes 3145732
  43.5 22.0 %collective-permute-start.2 = (f32[512]{0:T(512)S(1)}, f32[512]{0:T(512)S(1)}, u32[]{:S(2)}, u32[]{:S(2)}) collective-permute-start(f32[512]{0:T(512)S(1)} %get-tuple-element.32), channel_id=1, source_target_pairs={{1,0},{2,1},{3,2},{4,3},{5,4},{6,5},{7,6},{8,7},{9,8},{10,9},{11,1... | collective-permute-start | bytes 6152 | tf_op jit(solution)/shard_map/ppermute | solution.py:16
  46.1 6.3 %copy-start.5 = (bf16[512,1024]{1,0:T(8,128)(2,1)S(1)}, bf16[512,1024]{1,0:T(8,128)(2,1)}, u32[]{:S(2)}) copy-start(bf16[512,1024]{1,0:T(8,128)(2,1)} %param.9) | copy-start | bytes 3145732
  46.1 19.4 %collective-permute-start.3 = (f32[512]{0:T(512)S(1)}, f32[512]{0:T(512)S(1)}, u32[]{:S(2)}, u32[]{:S(2)}) collective-permute-start(f32[512]{0:T(512)S(1)} %get-tuple-element.30), channel_id=1, source_target_pairs={{1,0},{2,1},{3,2},{4,3},{5,4},{6,5},{7,6},{8,7},{9,8},{10,9},{11,1... | collective-permute-start | bytes 6152 | tf_op jit(solution)/shard_map/ppermute | solution.py:16
  52.4 1.5 %copy-start.3 = (bf16[1024,1024]{1,0:T(8,128)(2,1)}, bf16[1024,1024]{1,0:T(8,128)(2,1)S(1)}, u32[]{:S(2)}) copy-start(bf16[1024,1024]{1,0:T(8,128)(2,1)S(1)} %constant_dynamic-update-slice_fusion) | copy-start | bytes 6291460
  55.1 10.4 %collective-permute-start.5 = (f32[512]{0:T(512)S(1)}, f32[512]{0:T(512)S(1)}, u32[]{:S(2)}, u32[]{:S(2)}) collective-permute-start(f32[512]{0:T(512)S(1)} %slice.49), channel_id=1, source_target_pairs={{1,0},{2,1},{3,2},{4,3},{5,4},{6,5},{7,6},{8,7},{9,8},{10,9},{11,1... | collective-permute-start | bytes 6152 | tf_op jit(solution)/shard_map/ppermute | solution.py:16
  58.2 7.3 %collective-permute-start.4 = (f32[512]{0:T(512)S(1)}, f32[512]{0:T(512)S(1)}, u32[]{:S(2)}, u32[]{:S(2)}) collective-permute-start(f32[512]{0:T(512)S(1)} %slice.47), channel_id=1, source_target_pairs={{1,0},{2,1},{3,2},{4,3},{5,4},{6,5},{7,6},{8,7},{9,8},{10,9},{11,1... | collective-permute-start | bytes 6152 | tf_op jit(solution)/shard_map/ppermute | solution.py:16
  66.1 6.1 %collective-permute-start.7 = (f32[512]{0:T(512)S(1)}, f32[512]{0:T(512)S(1)}, u32[]{:S(2)}, u32[]{:S(2)}) collective-permute-start(f32[512]{0:T(512)S(1)} %get-tuple-element.40), channel_id=1, source_target_pairs={{0,1},{1,2},{2,3},{3,4},{4,5},{5,6},{6,7},{7,8},{8,9},{9,10},{10,1... | collective-permute-start | bytes 6152 | tf_op jit(solution)/shard_map/ppermute | solution.py:16
  68.8 9.4 %copy-start.6 = (bf16[512,1024]{1,0:T(8,128)(2,1)S(1)}, bf16[512,1024]{1,0:T(8,128)(2,1)}, u32[]{:S(2)}) copy-start(bf16[512,1024]{1,0:T(8,128)(2,1)} %param.9) | copy-start | bytes 3145732
  68.8 9.4 %collective-permute-start.6 = (f32[512]{0:T(512)S(1)}, f32[512]{0:T(512)S(1)}, u32[]{:S(2)}, u32[]{:S(2)}) collective-permute-start(f32[512]{0:T(512)S(1)} %get-tuple-element.34), channel_id=1, source_target_pairs={{0,1},{1,2},{2,3},{3,4},{4,5},{5,6},{6,7},{7,8},{8,9},{9,10},{10,1... | collective-permute-start | bytes 6152 | tf_op jit(solution)/shard_map/ppermute | solution.py:16
  74.6 37.7 %collective-permute-start.8 = (bf16[512,1024]{1,0:T(8,128)(2,1)S(1)}, bf16[512,1024]{1,0:T(8,128)(2,1)S(1)}, u32[]{:S(2)}, u32[]{:S(2)}) collective-permute-start(bf16[512,1024]{1,0:T(8,128)(2,1)S(1)} %convolution_convert_fusion), channel_id=1, source_target_pairs={{1,0},{2,1},{3,2},{4,3},{5,4},{6,5},{7,6},{8,7},{9,8},{10,9},{11,1... | collective-permute-start | bytes 3145736 | tf_op jit(solution)/shard_map/ppermute | solution.py:16
  80.0 32.3 %copy-start.4 = (bf16[1024,1024]{1,0:T(8,128)(2,1)S(1)}, bf16[1024,1024]{1,0:T(8,128)(2,1)}, u32[]{:S(2)}) copy-start(bf16[1024,1024]{1,0:T(8,128)(2,1)} %copy-done.3) | copy-start | bytes 6291460
  80.1 43.4 %copy-start.2 = (f32[512,512]{1,0:T(8,128)S(1)}, f32[512,512]{1,0:T(8,128)}, u32[]{:S(2)}) copy-start(f32[512,512]{1,0:T(8,128)} %copy-done.1) | copy-start | bytes 3145732
  80.2 43.4 %copy-start.8 = (bf16[512,1024]{1,0:T(8,128)(2,1)S(1)}, bf16[512,1024]{1,0:T(8,128)(2,1)}, u32[]{:S(2)}) copy-start(bf16[512,1024]{1,0:T(8,128)(2,1)} %copy-done.7) | copy-start | bytes 3145732
  80.2 43.4 %collective-permute-start.9 = (bf16[512,1024]{1,0:T(8,128)(2,1)S(1)}, bf16[512,1024]{1,0:T(8,128)(2,1)S(1)}, u32[]{:S(2)}, u32[]{:S(2)}) collective-permute-start(bf16[512,1024]{1,0:T(8,128)(2,1)S(1)} %slice.85), channel_id=1, source_target_pairs={{1,0},{2,1},{3,2},{4,3},{5,4},{6,5},{7,6},{8,7},{9,8},{10,9},{11,1... | collective-permute-start | bytes 3145736 | tf_op jit(solution)/shard_map/ppermute | solution.py:16
where the time goes:
time: 127 us; the launch traced here: 126 us
  waiting for transfers between devices  69.8 us (55%)
  starting transfers between devices  28.1 us (22%)
  matrix products  12.8 us (10%)
  other arithmetic  8.21 us (6%)
  local copies, waits for them, and re-layouts  5.59 us (4%)
    ppermute x10, waiting for transfers between devices, shifted_2(): return lax.ppermute(shard, axis, pairs)  69.8 us
    ppermute x10, starting transfers between devices, shifted_2(): return lax.ppermute(shard, axis, pairs)  28.1 us
    gather x1, local copies, waits for them, and re-layouts, shards(): diagonal = jnp.diagonal(scores_own[:, kept:])  4.55 us
    dot_general x2, matrix products, dot_rows(): lax.dot_general(former, latter, (((1,), (1,)), ((), ())), preferred_eleme...  3.89 us
    dot_general x2, matrix products, dot_cols(): lax.dot_general(former, latter, (((0,), (0,)), ((), ())), preferred_eleme...  3.82 us
    dot_general x1, matrix products, shards(): jnp.dot(grad_own, window_responses, preferred_element_type=jnp.float32)  2.73 us
    select_n x1, other arithmetic, shards(): jnp.repeat(left_blocks, BLK, total_repeat_length=row_count)[skipped:]  2.59 us
  transfers between devices with their start and end apart: 10, of which 5 were waited for; matrix products, arithmetic and copies ran while one was open for 19% of the time, Pallas kernels for 0%

commit v1 on v0

v1 whole, which is shorter than its diff:
```python
import jax
import jax.numpy as jnp
from jax import lax
from jax.experimental import pallas as pl
from jax.experimental.pallas import tpu as pltpu
from jax.sharding import PartitionSpec as P

MESH = pl.DeviceIdType.MESH
BLK = 128
ROWS = 512
D = 1024
HALF = 64
CHUNKS = 6
DEPTH = 3
SCALE = 20.0
MASKED = -1e30
F32 = jnp.float32
BF16 = jnp.bfloat16
BLOCKS = ROWS // BLK


def dot_rows(former, latter):
    return lax.dot_general(former, latter, (((1,), (1,)), ((), ())), preferred_element_type=F32)


def dot(former, latter):
    return jnp.dot(former, latter, preferred_element_type=F32)


def rows_of(b):
    return pl.ds(b * BLK, BLK)


def lanes(shape):
    return lax.broadcasted_iota(jnp.int32, shape, len(shape) - 1)


def eye():
    shape = (BLK, BLK)
    return lax.broadcasted_iota(jnp.int32, shape, 0) == lanes(shape)


def to_lanes(column):
    return jnp.sum(jnp.where(eye(), column, 0.0), axis=0, keepdims=True)


def wide(column):
    return jnp.broadcast_to(column[:, :1], (BLK, D))


def exchange(
    q_hbm, r_hbm, cluster_hbm,
    g1, g2, h1, e_own, r_own, m_col, z_col, m_first, bias, last_msg, last_q, loss_q, diag_out,
    q_own, held, s_own, t_own, x_ref, h2, m_row, z_row, msg_right, msg_left, got_left, got_right, ids,
    send_sem, recv_sem, msg_send, msg_recv, load_sem,
):
    shape_wide, shape_narrow = lax.axis_size("wide"), lax.axis_size("narrow")
    count = shape_wide * shape_narrow
    me = lax.axis_index("wide") * shape_narrow + lax.axis_index("narrow")
    left, right = lax.rem(me + count - 1, count), lax.rem(me + 1, count)

    def coords(p):
        return (p // shape_narrow, lax.rem(p, shape_narrow))

    loads = [
        pltpu.make_async_copy(q_hbm, q_own, load_sem.at[0]),
        pltpu.make_async_copy(r_hbm, r_own, load_sem.at[1]),
        pltpu.make_async_copy(cluster_hbm, ids, load_sem.at[2]),
    ]
    for load in loads:
        load.start()

    barrier = pltpu.get_barrier_semaphore()
    for p in (left, right):
        pl.semaphore_signal(barrier, inc=1, device_id=coords(p), device_id_type=MESH)
    pl.semaphore_wait(barrier, 2)

    def copies(src, slot, c):
        to_right = pltpu.make_async_remote_copy(
            src_ref=src.at[pl.ds(BLK + c * HALF, HALF)],
            dst_ref=held.at[slot, pl.ds(0, HALF)],
            send_sem=send_sem.at[slot, 0],
            recv_sem=recv_sem.at[slot, 0],
            device_id=coords(right),
            device_id_type=MESH,
        )
        to_left = pltpu.make_async_remote_copy(
            src_ref=src.at[pl.ds(c * HALF, HALF)],
            dst_ref=held.at[slot, pl.ds(HALF, HALF)],
            send_sem=send_sem.at[slot, 1],
            recv_sem=recv_sem.at[slot, 1],
            device_id=coords(left),
            device_id_type=MESH,
        )
        return to_right, to_left

    def start(src, slot, c):
        for copy in copies(src, slot, c):
            copy.start()

    def sent(src, slot, c):
        for copy in copies(src, slot, c):
            copy.wait_send()

    def landed(src, slot, c):
        for copy in copies(src, slot, c):
            copy.wait_recv()

    for c in range(DEPTH):
        start(r_hbm, c, c)

    for load in loads:
        load.wait()
    own_ids = [ids[me * BLOCKS + b] for b in range(BLOCKS)]
    lane = lanes((1, ROWS))
    id_row = jnp.full((1, ROWS), own_ids[0], jnp.int32)
    for b in range(1, BLOCKS):
        id_row = jnp.where(lane >= b * BLK, own_ids[b], id_row)

    for b in range(BLOCKS):
        allowed = jnp.broadcast_to(id_row == own_ids[b], (BLK, ROWS))
        s_own[rows_of(b)] = jnp.where(allowed, dot_rows(q_own[rows_of(b)], r_own[...]) * SCALE, MASKED)
        t_own[rows_of(b)] = jnp.where(allowed, dot_rows(r_own[rows_of(b)], q_own[...]) * SCALE, MASKED)

    def sums_by_lane(scores):
        largest = jnp.max(scores[...], axis=0, keepdims=True)
        return largest, jnp.sum(jnp.exp(scores[...] - largest), axis=0, keepdims=True)

    largest_cols, summed_cols = sums_by_lane(s_own)
    largest_rows, summed_rows = sums_by_lane(t_own)
    for k, lse in enumerate((largest_cols + jnp.log(summed_cols), largest_rows + jnp.log(summed_rows))):
        lse = jnp.broadcast_to(lse, (8, ROWS))
        ahead, behind = pltpu.roll(lse, ROWS - HALF, 1), pltpu.roll(lse, HALF, 1)
        for c in range(CHUNKS):
            at = (c // 2) * BLK
            row = pl.ds(8 * k + c, 1)
            msg_right[row] = (ahead if c % 2 else lse)[:1, BLK + at : 2 * BLK + at]
            msg_left[row] = (lse if c % 2 else behind)[:1, at : BLK + at]
        rest = pl.ds(8 * k + CHUNKS, 8 - CHUNKS)
        msg_right[rest] = jnp.zeros((8 - CHUNKS, BLK), F32)
        msg_left[rest] = jnp.zeros((8 - CHUNKS, BLK), F32)
    messages = [
        pltpu.make_async_remote_copy(
            src_ref=src,
            dst_ref=dst,
            send_sem=msg_send.at[k],
            recv_sem=msg_recv.at[k],
            device_id=coords(p),
            device_id_type=MESH,
        )
        for k, (src, dst, p) in enumerate(((msg_right, got_left, right), (msg_left, got_right, left)))
    ]
    for message in messages:
        message.start()

    def own_part(scores, other, m_ref, z_ref, total):
        for b in range(BLOCKS):
            x = scores[rows_of(b)]
            largest = jnp.max(x, axis=1, keepdims=True)
            e = jnp.exp(x - largest)
            m_ref[rows_of(b)] = jnp.broadcast_to(largest, (BLK, BLK))
            z_ref[rows_of(b)] = jnp.broadcast_to(jnp.sum(e, axis=1, keepdims=True), (BLK, BLK))
            total[rows_of(b)] = dot(e.astype(BF16), other[...])

    own_part(s_own, r_own, m_row, z_row, h1)
    own_part(t_own, q_own, m_col, z_col, g1)
    e_own[...] = jnp.exp(s_own[...] - largest_cols)
    m_first[...] = jnp.broadcast_to(largest_cols, (8, ROWS))
    h2[...] = jnp.zeros_like(h2)

    first_half = lanes((1, BLK)) < HALF

    def ids_of(c):
        return jnp.where(first_half, ids[left * BLOCKS + 1 + c // 2], ids[right * BLOCKS + c // 2])

    def message_of(row):
        return jnp.where(first_half, got_left[pl.ds(row, 1)], got_right[pl.ds(row, 1)])

    def chunk_part(c, slot, msg_row, own, m_ref, z_ref, scaled, total):
        chunk = held.at[slot]
        id_chunk = ids_of(c)
        for b in range(BLOCKS):
            allowed = jnp.broadcast_to(id_chunk == own_ids[b], (BLK, BLK))
            x_ref[rows_of(b)] = jnp.where(allowed, dot_rows(own[rows_of(b)], chunk[...]) * SCALE, MASKED)
        msg = message_of(msg_row)
        largest = jnp.maximum(jnp.max(x_ref[...], axis=0, keepdims=True), msg)
        summed = jnp.exp(msg - largest) + jnp.sum(jnp.exp(x_ref[...] - largest), axis=0, keepdims=True)
        lse = largest + jnp.log(summed)
        for b in range(BLOCKS):
            rows = rows_of(b)
            x = x_ref[rows]
            before = m_ref[rows]
            after = jnp.maximum(before, jnp.max(x, axis=1, keepdims=True))
            shrink = jnp.exp(before - after)
            e = jnp.exp(x - after)
            m_ref[rows] = after
            z_ref[rows] = z_ref[rows] * shrink + jnp.sum(e, axis=1, keepdims=True)
            scaled[rows] = scaled[rows] * wide(shrink) + dot(e.astype(BF16), chunk[...])
            total[rows] += dot(jnp.exp(x - lse).astype(BF16), chunk[...])

    for message in messages:
        message.wait()

    @pl.loop(0, CHUNKS)
    def _(c):
        sent(r_hbm, c, c)

        @pl.when(c < CHUNKS - DEPTH)
        def _():
            start(r_hbm, c + DEPTH, c + DEPTH)

        @pl.when(c >= CHUNKS - DEPTH)
        def _():
            start(q_hbm, c + DEPTH, c + DEPTH - CHUNKS)

        landed(r_hbm, c, c)
        chunk_part(c, c, c, q_own, m_row, z_row, h1, h2)

    row_lse = []
    diagonal = []
    for b in range(BLOCKS):
        rows = rows_of(b)
        z = z_row[rows]
        row_lse.append(to_lanes(m_row[rows] + jnp.log(z)))
        diagonal.append(to_lanes(s_own[rows, b * BLK : (b + 1) * BLK]))
        h1[rows] = h1[rows] * wide(1.0 / z) + h2[rows] - r_own[rows].astype(F32)
        loss_q[pl.ds(b, 1)] = row_lse[b] - diagonal[b]
        diag_out[pl.ds(b, 1)] = diagonal[b]
    row_lse = jnp.concatenate(row_lse, axis=1)
    for b in range(BLOCKS):
        rows = rows_of(b)
        at_diagonal = lanes((BLK, ROWS)) == lax.broadcasted_iota(jnp.int32, (BLK, ROWS), 0) + b * BLK
        w = jnp.exp(t_own[rows] - row_lse) - jnp.where(at_diagonal, 1.0, 0.0)
        g2[rows] = dot(w.astype(BF16), q_own[...]) - q_own[rows].astype(F32)

    @pl.loop(0, CHUNKS - 1)
    def _(c):
        sent(q_hbm, CHUNKS + c, c)

        @pl.when(c < CHUNKS - DEPTH)
        def _():
            start(q_hbm, CHUNKS + c + DEPTH, c + DEPTH)

        landed(q_hbm, CHUNKS + c, c)
        chunk_part(c, CHUNKS + c, 8 + c, r_own, m_col, z_col, g1, g2)

    c = CHUNKS - 1
    id_chunk = ids_of(c)
    for b in range(BLOCKS):
        allowed = jnp.broadcast_to(id_chunk == own_ids[b], (BLK, BLK))
        bias[rows_of(b)] = jnp.where(allowed, 0.0, MASKED)
    last_msg[...] = jnp.broadcast_to(message_of(8 + c), (8, BLK))
    sent(q_hbm, CHUNKS + c, c)
    landed(q_hbm, CHUNKS + c, c)
    last_q[...] = held[CHUNKS + c]


def finish(
    g1, g2, h1, e_own, r_own, m_col, z_col, m_first, bias, last_msg, last_q, loss_q, diagonal,
    loss_q_out, loss_r_out, q_out, r_out,
    x_ref, w_ref, gq, gr, sems,
):
    for b in range(BLOCKS):
        rows = rows_of(b)
        x = dot_rows(r_own[rows], last_q[...]) * SCALE
        x_ref[rows] = jnp.where(bias[rows] < 0.0, MASKED, x)
    msg = last_msg[:1]
    largest = jnp.maximum(jnp.max(x_ref[...], axis=0, keepdims=True), msg)
    summed = jnp.exp(msg - largest) + jnp.sum(jnp.exp(x_ref[...] - largest), axis=0, keepdims=True)
    row_lse = largest + jnp.log(summed)
    loss_q_out[...] = loss_q[...]
    factors = []
    copies = []
    for b in range(BLOCKS):
        rows = rows_of(b)
        x = x_ref[rows]
        before = m_col[rows]
        after = jnp.maximum(before, jnp.max(x, axis=1, keepdims=True))
        shrink = jnp.exp(before - after)
        e = jnp.exp(x - after)
        z = z_col[rows] * shrink + jnp.sum(e, axis=1, keepdims=True)
        inverse = 1.0 / z
        col_lse = to_lanes(after + jnp.log(z))
        loss_r_out[pl.ds(b, 1)] = col_lse - diagonal[pl.ds(b, 1)]
        factors.append(jnp.exp(m_first[:1, b * BLK : (b + 1) * BLK] - col_lse))
        w = e * inverse + jnp.exp(x - row_lse)
        total = g1[rows] * wide(shrink * inverse) + g2[rows] + dot(w.astype(BF16), last_q[...])
        gr[rows] = (total * SCALE).astype(BF16)
        copies.append(pltpu.make_async_copy(gr.at[rows], r_out.at[rows], sems.at[b]))
        copies[-1].start()
    factors = jnp.concatenate(factors, axis=1)
    for b in range(BLOCKS):
        rows = rows_of(b)
        at_diagonal = lanes((BLK, ROWS)) == lax.broadcasted_iota(jnp.int32, (BLK, ROWS), 0) + b * BLK
        w = e_own[rows] * factors - jnp.where(at_diagonal, 1.0, 0.0)
        total = h1[rows] + dot(w.astype(BF16), r_own[...])
        gq[rows] = (total * SCALE).astype(BF16)
        copies.append(pltpu.make_async_copy(gq.at[rows], q_out.at[rows], sems.at[BLOCKS + b]))
        copies[-1].start()
    for copy in copies:
        copy.wait()


def shards(queries, responses, block_cluster):
    queries, responses, block_cluster = (
        pltpu.with_memory_space_constraint(a, pltpu.HBM) for a in (queries, responses, block_cluster)
    )
    vmem = pl.BlockSpec(memory_space=pltpu.VMEM)
    hbm = pl.BlockSpec(memory_space=pltpu.HBM)
    passed = (
        ((ROWS, D), F32),
        ((ROWS, D), F32),
        ((ROWS, D), F32),
        ((ROWS, ROWS), F32),
        ((ROWS, D), BF16),
        ((ROWS, BLK), F32),
        ((ROWS, BLK), F32),
        ((8, ROWS), F32),
        ((ROWS, BLK), F32),
        ((8, BLK), F32),
        ((BLK, D), BF16),
        ((BLOCKS, BLK), F32),
        ((BLOCKS, BLK), F32),
    )
    parts = pl.pallas_call(
        exchange,
        out_shape=[pltpu.VMEM(shape, dtype) for shape, dtype in passed],
        in_specs=[hbm] * 3,
        out_specs=[vmem] * len(passed),
        scratch_shapes=[
            pltpu.VMEM((ROWS, D), BF16),
            pltpu.VMEM((2 * CHUNKS, BLK, D), BF16),
            pltpu.VMEM((ROWS, ROWS), F32),
            pltpu.VMEM((ROWS, ROWS), F32),
            pltpu.VMEM((ROWS, BLK), F32),
            pltpu.VMEM((ROWS, D), F32),
            pltpu.VMEM((ROWS, BLK), F32),
            pltpu.VMEM((ROWS, BLK), F32),
            pltpu.VMEM((16, BLK), F32),
            pltpu.VMEM((16, BLK), F32),
            pltpu.VMEM((16, BLK), F32),
            pltpu.VMEM((16, BLK), F32),
            pltpu.SMEM(block_cluster.shape, jnp.int32),
            pltpu.SemaphoreType.DMA((2 * CHUNKS, 2)),
            pltpu.SemaphoreType.DMA((2 * CHUNKS, 2)),
            pltpu.SemaphoreType.DMA((2,)),
            pltpu.SemaphoreType.DMA((2,)),
            pltpu.SemaphoreType.DMA((3,)),
        ],
        compiler_params=pltpu.CompilerParams(
            collective_id=0, has_side_effects=True, vmem_limit_bytes=32 * 2**20
        ),
        name="exchange",
    )(queries, responses, block_cluster)
    query_loss, response_loss, query_grad, response_grad = pl.pallas_call(
        finish,
        out_shape=[
            jax.ShapeDtypeStruct((BLOCKS, BLK), F32),
            jax.ShapeDtypeStruct((BLOCKS, BLK), F32),
            jax.ShapeDtypeStruct((ROWS, D), BF16),
            jax.ShapeDtypeStruct((ROWS, D), BF16),
        ],
        in_specs=[vmem] * len(passed),
        out_specs=[vmem, vmem, hbm, hbm],
        scratch_shapes=[
            pltpu.VMEM((ROWS, BLK), F32),
            pltpu.VMEM((ROWS, BLK), BF16),
            pltpu.VMEM((ROWS, D), BF16),
            pltpu.VMEM((ROWS, D), BF16),
            pltpu.SemaphoreType.DMA((2 * BLOCKS,)),
        ],
        compiler_params=pltpu.CompilerParams(vmem_limit_bytes=32 * 2**20),
        name="finish",
    )(*parts)
    return query_loss.reshape(ROWS), response_loss.reshape(ROWS), query_grad, response_grad


def solution(mesh):
    both = ("wide", "narrow")
    return jax.shard_map(
        shards,
        mesh=mesh,
        in_specs=(P(both, None), P(both, None), P()),
        out_specs=(P(both), P(both), P(both, None), P(both, None)),
        check_vma=False,
    )
```

time: 127 us -> 52.6 us (0.41)
  the two profiles are of different devices: /device:TPU:481 before, /device:TPU:1 now
where the time goes in v1:
time: 52.6 us; the launch traced here: 52.4 us
  Pallas kernels  51.8 us (98%)
  between operations  0.64 us (1%)
    pallas_call x1, Pallas kernels, shards(): pl.pallas_call(exchange, out_shape=[pltpu.VMEM(shape, dtype) for shape, d...  48.5 us
    pallas_call x1, Pallas kernels, shards(): pl.pallas_call(finish, out_shape=[jax.ShapeDtypeStruct((BLOCKS, BLK), F32...  3.28 us

profile of v1, /device:TPU:1, one launch (start us, length us, event | category | flops | bytes accessed | tf_op | source)
XLA Modules:
  0.0 52.4 jit_solution(14593775569961726339)
XLA Ops:
  0.6 48.5 %exchange.1 = (f32[512,1024]{1,0:T(8,128)S(1)}, f32[512,1024]{1,0:T(8,128)S(1)}, f32[512,1024]{1,0:T(8,128)S(1)}, f32[512,512]{1,0:T(8,128)S(1)}, bf16[512,1024]...) custom-call(bf16[512,1024]{1,0:T(8,128)(2,1)} %q_hbm.1, ...), custom_call_target="tpu_custom_call" | custom-call | tf_op jit(solution)/shard_map/exchange/pallas_call | solution.py:325
  49.2 3.3 %finish.1 = (f32[4,128]{1,0:T(4,128)}, f32[4,128]{1,0:T(4,128)}, bf16[512,1024]{1,0:T(8,128)(2,1)}, bf16[512,1024]{1,0:T(8,128)(2,1)}) custom-call(f32[512,1024]{1,0:T(8,128)S(1)} %get-tuple-element.21.g1, f32[512,1024]{1,0:T(8,128)S(1)} %get-tuple-element.22.g2, f32[512,1024]{1,0:T(8,128)S(1)} %get-tuple-element.23.h1, ...), custom_call_target="tpu_custom_call" | custom-call | tf_op jit(solution)/shard_map/finish/pallas_call | solution.py:355

commit v2 on v1

--- a/solution.py
+++ b/solution.py
@@ -11,7 +11,6 @@
 D = 1024
 HALF = 64
 CHUNKS = 6
-DEPTH = 3
 SCALE = 20.0
 MASKED = -1e30
 F32 = jnp.float32
@@ -51,7 +50,7 @@
 def exchange(
     q_hbm, r_hbm, cluster_hbm,
     g1, g2, h1, e_own, r_own, m_col, z_col, m_first, bias, last_msg, last_q, loss_q, diag_out,
-    q_own, held, s_own, t_own, x_ref, h2, m_row, z_row, msg_right, msg_left, got_left, got_right, ids,
+    q_own, held, s_own, t_own, x_ref, msg_right, msg_left, got_left, got_right, ids,
     send_sem, recv_sem, msg_send, msg_recv, load_sem,
 ):
     shape_wide, shape_narrow = lax.axis_size("wide"), lax.axis_size("narrow")
@@ -98,15 +97,11 @@
         for copy in copies(src, slot, c):
             copy.start()
 
-    def sent(src, slot, c):
-        for copy in copies(src, slot, c):
-            copy.wait_send()
-
     def landed(src, slot, c):
         for copy in copies(src, slot, c):
             copy.wait_recv()
 
-    for c in range(DEPTH):
+    for c in range(CHUNKS):
         start(r_hbm, c, c)
 
     for load in loads:
@@ -152,113 +147,115 @@
     ]
     for message in messages:
         message.start()
-
-    def own_part(scores, other, m_ref, z_ref, total):
-        for b in range(BLOCKS):
-            x = scores[rows_of(b)]
-            largest = jnp.max(x, axis=1, keepdims=True)
-            e = jnp.exp(x - largest)
-            m_ref[rows_of(b)] = jnp.broadcast_to(largest, (BLK, BLK))
-            z_ref[rows_of(b)] = jnp.broadcast_to(jnp.sum(e, axis=1, keepdims=True), (BLK, BLK))
-            total[rows_of(b)] = dot(e.astype(BF16), other[...])
-
-    own_part(s_own, r_own, m_row, z_row, h1)
-    own_part(t_own, q_own, m_col, z_col, g1)
+    for c in range(CHUNKS):
+        start(q_hbm, CHUNKS + c, c)
+
+    for b in range(BLOCKS):
+        rows = rows_of(b)
+        x = t_own[rows]
+        largest = jnp.max(x, axis=1, keepdims=True)
+        e = jnp.exp(x - largest)
+        m_col[rows] = jnp.broadcast_to(largest, (BLK, BLK))
+        z_col[rows] = jnp.broadcast_to(jnp.sum(e, axis=1, keepdims=True), (BLK, BLK))
+        g1[rows] = dot(e.astype(BF16), q_own[...])
     e_own[...] = jnp.exp(s_own[...] - largest_cols)
     m_first[...] = jnp.broadcast_to(largest_cols, (8, ROWS))
-    h2[...] = jnp.zeros_like(h2)
 
     first_half = lanes((1, BLK)) < HALF
 
     def ids_of(c):
         return jnp.where(first_half, ids[left * BLOCKS + 1 + c // 2], ids[right * BLOCKS + c // 2])
 
-    def message_of(row):
-        return jnp.where(first_half, got_left[pl.ds(row, 1)], got_right[pl.ds(row, 1)])
-
-    def chunk_part(c, slot, msg_row, own, m_ref, z_ref, scaled, total):
-        chunk = held.at[slot]
+    def scores_of(c, slot, own):
         id_chunk = ids_of(c)
         for b in range(BLOCKS):
             allowed = jnp.broadcast_to(id_chunk == own_ids[b], (BLK, BLK))
-            x_ref[rows_of(b)] = jnp.where(allowed, dot_rows(own[rows_of(b)], chunk[...]) * SCALE, MASKED)
-        msg = message_of(msg_row)
-        largest = jnp.maximum(jnp.max(x_ref[...], axis=0, keepdims=True), msg)
-        summed = jnp.exp(msg - largest) + jnp.sum(jnp.exp(x_ref[...] - largest), axis=0, keepdims=True)
+            x_ref[c, rows_of(b)] = jnp.where(allowed, dot_rows(own[rows_of(b)], held[slot]) * SCALE, MASKED)
+
+    def lse_of(c, msg_row):
+        x = x_ref[c]
+        msg = jnp.where(first_half, got_left[pl.ds(msg_row, 1)], got_right[pl.ds(msg_row, 1)])
+        largest = jnp.maximum(jnp.max(x, axis=0, keepdims=True), msg)
+        summed = jnp.exp(msg - largest) + jnp.sum(jnp.exp(x - largest), axis=0, keepdims=True)
+        return largest + jnp.log(summed)
+
+    def at_diagonal(b):
+        shape = (BLK, ROWS)
+        return lanes(shape) == lax.broadcasted_iota(jnp.int32, shape, 0) + b * BLK
+
+    @pl.loop(0, CHUNKS)
+    def _(c):
+        landed(r_hbm, c, c)
+        scores_of(c, c, q_own)
+
+    for message in messages:
+        message.wait()
+    col_lse = jnp.concatenate([lse_of(c, c) for c in range(CHUNKS)], axis=1)
+    row_lse = []
+    for b in range(BLOCKS):
+        rows = rows_of(b)
+        own = s_own[rows]
+        others = jnp.concatenate([x_ref[c, rows] for c in range(CHUNKS)], axis=1)
+        largest = jnp.maximum(jnp.max(own, axis=1, keepdims=True), jnp.max(others, axis=1, keepdims=True))
+        summed = jnp.sum(jnp.exp(own - largest), axis=1, keepdims=True)
+        summed += jnp.sum(jnp.exp(others - largest), axis=1, keepdims=True)
         lse = largest + jnp.log(summed)
+        w_own = jnp.exp(own - lse) - jnp.where(at_diagonal(b), 1.0, 0.0)
+        w_others = jnp.exp(others - lse) + jnp.exp(others - col_lse)
+        h1[rows] = dot(w_own.astype(BF16), r_own[...]) + dot(
+            w_others.astype(BF16), held[:CHUNKS].reshape(CHUNKS * BLK, D)
+        )
+        row_lse.append(to_lanes(lse))
+        diagonal = to_lanes(s_own[rows, b * BLK : (b + 1) * BLK])
+        loss_q[pl.ds(b, 1)] = row_lse[b] - diagonal
+        diag_out[pl.ds(b, 1)] = diagonal
+    row_lse = jnp.concatenate(row_lse, axis=1)
+    for b in range(BLOCKS):
+        rows = rows_of(b)
+        w = jnp.exp(t_own[rows] - row_lse) - jnp.where(at_diagonal(b), 1.0, 0.0)
+        g2[rows] = dot(w.astype(BF16), q_own[...]) - q_own[rows].astype(F32)
+
+    for first, end in ((0, CHUNKS // 2), (CHUNKS // 2, CHUNKS - 1)):
+
+        @pl.loop(first, end)
+        def _(c):
+            landed(q_hbm, CHUNKS + c, c)
+            scores_of(c, CHUNKS + c, r_own)
+
+        group = range(first, end)
+        lse = jnp.concatenate([lse_of(c, 8 + c) for c in group], axis=1)
         for b in range(BLOCKS):
             rows = rows_of(b)
-            x = x_ref[rows]
-            before = m_ref[rows]
+            x = jnp.concatenate([x_ref[c, rows] for c in group], axis=1)
+            before = m_col[rows]
             after = jnp.maximum(before, jnp.max(x, axis=1, keepdims=True))
             shrink = jnp.exp(before - after)
-            e = jnp.exp(x - after)
-            m_ref[rows] = after
-            z_ref[rows] = z_ref[rows] * shrink + jnp.sum(e, axis=1, keepdims=True)
-            scaled[rows] = scaled[rows] * wide(shrink) + dot(e.astype(BF16), chunk[...])
-            total[rows] += dot(jnp.exp(x - lse).astype(BF16), chunk[...])
-
-    for message in messages:
-        message.wait()
-
-    @pl.loop(0, CHUNKS)
-    def _(c):
-        sent(r_hbm, c, c)
-
-        @pl.when(c < CHUNKS - DEPTH)
-        def _():
-            start(r_hbm, c + DEPTH, c + DEPTH)
-
-        @pl.when(c >= CHUNKS - DEPTH)
-        def _():
-            start(q_hbm, c + DEPTH, c + DEPTH - CHUNKS)
-
-        landed(r_hbm, c, c)
-        chunk_part(c, c, c, q_own, m_row, z_row, h1, h2)
-
-    row_lse = []
-    diagonal = []
-    for b in range(BLOCKS):
-        rows = rows_of(b)
-        z = z_row[rows]
-        row_lse.append(to_lanes(m_row[rows] + jnp.log(z)))
-        diagonal.append(to_lanes(s_own[rows, b * BLK : (b + 1) * BLK]))
-        h1[rows] = h1[rows] * wide(1.0 / z) + h2[rows] - r_own[rows].astype(F32)
-        loss_q[pl.ds(b, 1)] = row_lse[b] - diagonal[b]
-        diag_out[pl.ds(b, 1)] = diagonal[b]
-    row_lse = jnp.concatenate(row_lse, axis=1)
-    for b in range(BLOCKS):
-        rows = rows_of(b)
-        at_diagonal = lanes((BLK, ROWS)) == lax.broadcasted_iota(jnp.int32, (BLK, ROWS), 0) + b * BLK
-        w = jnp.exp(t_own[rows] - row_lse) - jnp.where(at_diagonal, 1.0, 0.0)
-        g2[rows] = dot(w.astype(BF16), q_own[...]) - q_own[rows].astype(F32)
-
-    @pl.loop(0, CHUNKS - 1)
-    def _(c):
-        sent(q_hbm, CHUNKS + c, c)
-
-        @pl.when(c < CHUNKS - DEPTH)
-        def _():
-            start(q_hbm, CHUNKS + c + DEPTH, c + DEPTH)
-
-        landed(q_hbm, CHUNKS + c, c)
-        chunk_part(c, CHUNKS + c, 8 + c, r_own, m_col, z_col, g1, g2)
+            e = jnp.exp(x - after[:, :1])
+            m_col[rows] = after
+            z_col[rows] = z_col[rows] * shrink + jnp.sum(e, axis=1, keepdims=True)
+            queries = held[CHUNKS + first : CHUNKS + end].reshape(len(group) * BLK, D)
+            g1[rows] = g1[rows] * wide(shrink) + dot(e.astype(BF16), queries)
+            g2[rows] += dot(jnp.exp(x - lse).astype(BF16), queries)
 
     c = CHUNKS - 1
     id_chunk = ids_of(c)
     for b in range(BLOCKS):
         allowed = jnp.broadcast_to(id_chunk == own_ids[b], (BLK, BLK))
         bias[rows_of(b)] = jnp.where(allowed, 0.0, MASKED)
-    last_msg[...] = jnp.broadcast_to(message_of(8 + c), (8, BLK))
-    sent(q_hbm, CHUNKS + c, c)
+    row = pl.ds(8 + c, 1)
+    last_msg[...] = jnp.broadcast_to(jnp.where(first_half, got_left[row], got_right[row]), (8, BLK))
     landed(q_hbm, CHUNKS + c, c)
     last_q[...] = held[CHUNKS + c]
+    for c in range(CHUNKS):
+        for src, slot in ((r_hbm, c), (q_hbm, CHUNKS + c)):
+            for copy in copies(src, slot, c):
+                copy.wait_send()
 
 
 def finish(
     g1, g2, h1, e_own, r_own, m_col, z_col, m_first, bias, last_msg, last_q, loss_q, diagonal,
     loss_q_out, loss_r_out, q_out, r_out,
-    x_ref, w_ref, gq, gr, sems,
+    x_ref, gq, gr, sems,
 ):
     for b in range(BLOCKS):
         rows = rows_of(b)
@@ -332,10 +329,7 @@
             pltpu.VMEM((2 * CHUNKS, BLK, D), BF16),
             pltpu.VMEM((ROWS, ROWS), F32),
             pltpu.VMEM((ROWS, ROWS), F32),
-            pltpu.VMEM((ROWS, BLK), F32),
-            pltpu.VMEM((ROWS, D), F32),
-            pltpu.VMEM((ROWS, BLK), F32),
-            pltpu.VMEM((ROWS, BLK), F32),
+            pltpu.VMEM((CHUNKS, ROWS, BLK), F32),
             pltpu.VMEM((16, BLK), F32),
             pltpu.VMEM((16, BLK), F32),
             pltpu.VMEM((16, BLK), F32),
@@ -364,7 +358,6 @@
         out_specs=[vmem, vmem, hbm, hbm],
         scratch_shapes=[
             pltpu.VMEM((ROWS, BLK), F32),
-            pltpu.VMEM((ROWS, BLK), BF16),
             pltpu.VMEM((ROWS, D), BF16),
             pltpu.VMEM((ROWS, D), BF16),
             pltpu.SemaphoreType.DMA((2 * BLOCKS,)),

time: 52.6 us -> 45.7 us (0.87)
  Pallas kernels: 51.8 us -> 45 us
    pallas_call x1, Pallas kernels: 48.5 us -> 41.7 us  [shards(): pl.pallas_call(exchange, out_shape=[pltpu.VMEM(shape, dtype) for shape, d...]
where the time goes in v2:
time: 45.7 us; the launch traced here: 45.6 us
  Pallas kernels  45 us (98%)
  between operations  0.64 us (1%)
    pallas_call x1, Pallas kernels, shards(): pl.pallas_call(exchange, out_shape=[pltpu.VMEM(shape, dtype) for shape, d...  41.7 us
    pallas_call x1, Pallas kernels, shards(): pl.pallas_call(finish, out_shape=[jax.ShapeDtypeStruct((BLOCKS, BLK), F32...  3.27 us

profile of v2, /device:TPU:1, one launch (start us, length us, event | category | flops | bytes accessed | tf_op | source)
XLA Modules:
  0.0 45.6 jit_solution(10788525693038087100)
XLA Ops:
  0.6 41.7 %exchange.1 = (f32[512,1024]{1,0:T(8,128)S(1)}, f32[512,1024]{1,0:T(8,128)S(1)}, f32[512,1024]{1,0:T(8,128)S(1)}, f32[512,512]{1,0:T(8,128)S(1)}, bf16[512,1024]...) custom-call(bf16[512,1024]{1,0:T(8,128)(2,1)} %q_hbm.1, ...), custom_call_target="tpu_custom_call" | custom-call | tf_op jit(solution)/shard_map/exchange/pallas_call | solution.py:322
  42.3 3.3 %finish.1 = (f32[4,128]{1,0:T(4,128)}, f32[4,128]{1,0:T(4,128)}, bf16[512,1024]{1,0:T(8,128)(2,1)}, bf16[512,1024]{1,0:T(8,128)(2,1)}) custom-call(f32[512,1024]{1,0:T(8,128)S(1)} %get-tuple-element.21.g1, f32[512,1024]{1,0:T(8,128)S(1)} %get-tuple-element.22.g2, f32[512,1024]{1,0:T(8,128)S(1)} %get-tuple-element.23.h1, ...), custom_call_target="tpu_custom_call" | custom-call | tf_op jit(solution)/shard_map/finish/pallas_call | solution.py:349

commit v3 on v2

--- a/solution.py
+++ b/solution.py
@@ -1,3 +1,5 @@
+import math
+
 import jax
 import jax.numpy as jnp
 from jax import lax
@@ -12,6 +14,9 @@
 HALF = 64
 CHUNKS = 6
 SCALE = 20.0
+LOG_SCALE = math.log(SCALE)
+PARTS = 2
+WIDTH = D // PARTS
 MASKED = -1e30
 F32 = jnp.float32
 BF16 = jnp.bfloat16
@@ -49,8 +54,8 @@
 
 def exchange(
     q_hbm, r_hbm, cluster_hbm,
-    g1, g2, h1, e_own, r_own, m_col, z_col, m_first, bias, last_msg, last_q, loss_q, diag_out,
-    q_own, held, s_own, t_own, x_ref, msg_right, msg_left, got_left, got_right, ids,
+    g1, g2, h1, e_own, r_own, scale_g1, factors, w_last, last_q, loss_q, loss_r,
+    q_own, m_col, z_col, held, s_own, t_own, x_ref, msg_right, msg_left, got_left, got_right, ids,
     send_sem, recv_sem, msg_send, msg_recv, load_sem,
 ):
     shape_wide, shape_narrow = lax.axis_size("wide"), lax.axis_size("narrow")
@@ -59,25 +64,32 @@
     left, right = lax.rem(me + count - 1, count), lax.rem(me + 1, count)
 
     def coords(p):
-        return (p // shape_narrow, lax.rem(p, shape_narrow))
+        return (lax.div(p, shape_narrow), lax.rem(p, shape_narrow))
 
     loads = [
         pltpu.make_async_copy(q_hbm, q_own, load_sem.at[0]),
         pltpu.make_async_copy(r_hbm, r_own, load_sem.at[1]),
         pltpu.make_async_copy(cluster_hbm, ids, load_sem.at[2]),
     ]
-    for load in loads:
-        load.start()
-
+    has_left, has_right = me > 0, me < count - 1
     barrier = pltpu.get_barrier_semaphore()
-    for p in (left, right):
-        pl.semaphore_signal(barrier, inc=1, device_id=coords(p), device_id_type=MESH)
-    pl.semaphore_wait(barrier, 2)
+    for p, exists in ((left, has_left), (right, has_right)):
+
+        @pl.when(exists)
+        def _():
+            pl.semaphore_signal(barrier, inc=1, device_id=coords(p), device_id_type=MESH)
+
+    for inner, signals in ((has_left & has_right, 2), (jnp.logical_not(has_left & has_right), 1)):
+
+        @pl.when(inner)
+        def _():
+            pl.semaphore_wait(barrier, signals)
 
     def copies(src, slot, c):
+        landing = last_q if isinstance(slot, int) and slot == 2 * CHUNKS - 1 else held.at[slot]
         to_right = pltpu.make_async_remote_copy(
             src_ref=src.at[pl.ds(BLK + c * HALF, HALF)],
-            dst_ref=held.at[slot, pl.ds(0, HALF)],
+            dst_ref=landing.at[pl.ds(0, HALF)],
             send_sem=send_sem.at[slot, 0],
             recv_sem=recv_sem.at[slot, 0],
             device_id=coords(right),
@@ -85,7 +97,7 @@
         )
         to_left = pltpu.make_async_remote_copy(
             src_ref=src.at[pl.ds(c * HALF, HALF)],
-            dst_ref=held.at[slot, pl.ds(HALF, HALF)],
+            dst_ref=landing.at[pl.ds(HALF, HALF)],
             send_sem=send_sem.at[slot, 1],
             recv_sem=recv_sem.at[slot, 1],
             device_id=coords(left),
@@ -93,16 +105,40 @@
         )
         return to_right, to_left
 
+    def started(pair):
+        to_right, to_left = pair
+        pl.when(has_right)(to_right.start)
+        pl.when(has_left)(to_left.start)
+
+    def received(pair):
+        from_left, from_right = pair
+        pl.when(has_left)(from_left.wait_recv)
+        pl.when(has_right)(from_right.wait_recv)
+
+    def sent(pair):
+        to_right, to_left = pair
+        pl.when(has_right)(to_right.wait_send)
+        pl.when(has_left)(to_left.wait_send)
+
     def start(src, slot, c):
-        for copy in copies(src, slot, c):
-            copy.start()
+        started(copies(src, slot, c))
 
     def landed(src, slot, c):
-        for copy in copies(src, slot, c):
-            copy.wait_recv()
-
-    for c in range(CHUNKS):
+        received(copies(src, slot, c))
+
+    start(r_hbm, 0, 0)
+    for load in loads:
+        load.start()
+    for c in range(1, CHUNKS):
         start(r_hbm, c, c)
+
+    for exists, at, got in ((has_left, 0, got_left), (has_right, HALF, got_right)):
+
+        @pl.when(jnp.logical_not(exists))
+        def _():
+            held[:, pl.ds(at, HALF)] = jnp.zeros((2 * CHUNKS - 1, HALF, D), BF16)
+            last_q[pl.ds(at, HALF)] = jnp.zeros((HALF, D), BF16)
+            got[...] = jnp.zeros_like(got)
 
     for load in loads:
         load.wait()
@@ -145,8 +181,7 @@
         )
         for k, (src, dst, p) in enumerate(((msg_right, got_left, right), (msg_left, got_right, left)))
     ]
-    for message in messages:
-        message.start()
+    started(messages)
     for c in range(CHUNKS):
         start(q_hbm, CHUNKS + c, c)
 
@@ -159,18 +194,17 @@
         z_col[rows] = jnp.broadcast_to(jnp.sum(e, axis=1, keepdims=True), (BLK, BLK))
         g1[rows] = dot(e.astype(BF16), q_own[...])
     e_own[...] = jnp.exp(s_own[...] - largest_cols)
-    m_first[...] = jnp.broadcast_to(largest_cols, (8, ROWS))
 
     first_half = lanes((1, BLK)) < HALF
 
     def ids_of(c):
         return jnp.where(first_half, ids[left * BLOCKS + 1 + c // 2], ids[right * BLOCKS + c // 2])
 
-    def scores_of(c, slot, own):
+    def scores_of(c, chunk, own):
         id_chunk = ids_of(c)
         for b in range(BLOCKS):
             allowed = jnp.broadcast_to(id_chunk == own_ids[b], (BLK, BLK))
-            x_ref[c, rows_of(b)] = jnp.where(allowed, dot_rows(own[rows_of(b)], held[slot]) * SCALE, MASKED)
+            x_ref[c, rows_of(b)] = jnp.where(allowed, dot_rows(own[rows_of(b)], chunk[...]) * SCALE, MASKED)
 
     def lse_of(c, msg_row):
         x = x_ref[c]
@@ -186,12 +220,11 @@
     @pl.loop(0, CHUNKS)
     def _(c):
         landed(r_hbm, c, c)
-        scores_of(c, c, q_own)
-
-    for message in messages:
-        message.wait()
+        scores_of(c, held.at[c], q_own)
+
+    received(messages)
     col_lse = jnp.concatenate([lse_of(c, c) for c in range(CHUNKS)], axis=1)
-    row_lse = []
+    row_lse, diagonals = [], []
     for b in range(BLOCKS):
         rows = rows_of(b)
         own = s_own[rows]
@@ -202,25 +235,25 @@
         lse = largest + jnp.log(summed)
         w_own = jnp.exp(own - lse) - jnp.where(at_diagonal(b), 1.0, 0.0)
         w_others = jnp.exp(others - lse) + jnp.exp(others - col_lse)
-        h1[rows] = dot(w_own.astype(BF16), r_own[...]) + dot(
-            w_others.astype(BF16), held[:CHUNKS].reshape(CHUNKS * BLK, D)
+        h1[rows] = SCALE * (
+            dot(w_own.astype(BF16), r_own[...])
+            + dot(w_others.astype(BF16), held[:CHUNKS].reshape(CHUNKS * BLK, D))
         )
         row_lse.append(to_lanes(lse))
-        diagonal = to_lanes(s_own[rows, b * BLK : (b + 1) * BLK])
-        loss_q[pl.ds(b, 1)] = row_lse[b] - diagonal
-        diag_out[pl.ds(b, 1)] = diagonal
+        diagonals.append(to_lanes(s_own[rows, b * BLK : (b + 1) * BLK]))
+        loss_q[pl.ds(b, 1)] = row_lse[b] - diagonals[b]
     row_lse = jnp.concatenate(row_lse, axis=1)
     for b in range(BLOCKS):
         rows = rows_of(b)
         w = jnp.exp(t_own[rows] - row_lse) - jnp.where(at_diagonal(b), 1.0, 0.0)
-        g2[rows] = dot(w.astype(BF16), q_own[...]) - q_own[rows].astype(F32)
+        g2[rows] = SCALE * (dot(w.astype(BF16), q_own[...]) - q_own[rows].astype(F32))
 
     for first, end in ((0, CHUNKS // 2), (CHUNKS // 2, CHUNKS - 1)):
 
         @pl.loop(first, end)
         def _(c):
             landed(q_hbm, CHUNKS + c, c)
-            scores_of(c, CHUNKS + c, r_own)
+            scores_of(c, held.at[CHUNKS + c], r_own)
 
         group = range(first, end)
         lse = jnp.concatenate([lse_of(c, 8 + c) for c in group], axis=1)
@@ -235,67 +268,77 @@
             z_col[rows] = z_col[rows] * shrink + jnp.sum(e, axis=1, keepdims=True)
             queries = held[CHUNKS + first : CHUNKS + end].reshape(len(group) * BLK, D)
             g1[rows] = g1[rows] * wide(shrink) + dot(e.astype(BF16), queries)
-            g2[rows] += dot(jnp.exp(x - lse).astype(BF16), queries)
+            g2[rows] += dot(jnp.exp(x - (lse - LOG_SCALE)).astype(BF16), queries)
 
     c = CHUNKS - 1
-    id_chunk = ids_of(c)
-    for b in range(BLOCKS):
-        allowed = jnp.broadcast_to(id_chunk == own_ids[b], (BLK, BLK))
-        bias[rows_of(b)] = jnp.where(allowed, 0.0, MASKED)
-    row = pl.ds(8 + c, 1)
-    last_msg[...] = jnp.broadcast_to(jnp.where(first_half, got_left[row], got_right[row]), (8, BLK))
+    before = jnp.concatenate([to_lanes(m_col[rows_of(b)]) for b in range(BLOCKS)], axis=1)
+    z_before = jnp.concatenate([to_lanes(z_col[rows_of(b)]) for b in range(BLOCKS)], axis=1)
+    msg = jnp.where(first_half, got_left[pl.ds(8 + c, 1)], got_right[pl.ds(8 + c, 1)])
+    msg = jnp.sum(jnp.where(eye(), msg, 0.0), axis=1, keepdims=True)
+    shape = (BLK, ROWS)
+    id_chunk = jnp.where(
+        lax.broadcasted_iota(jnp.int32, shape, 0) < HALF, ids[left * BLOCKS + 1 + c // 2], ids[right * BLOCKS + c // 2]
+    )
+    allowed = id_chunk == jnp.broadcast_to(id_row, shape)
     landed(q_hbm, CHUNKS + c, c)
-    last_q[...] = held[CHUNKS + c]
+    x = jnp.where(allowed, dot_rows(last_q[...], r_own[...]) * SCALE, MASKED)
+    after = jnp.maximum(before, jnp.max(x, axis=0, keepdims=True))
+    shrink = jnp.exp(before - after)
+    e = jnp.exp(x - after)
+    z = z_before * shrink + jnp.sum(e, axis=0, keepdims=True)
+    inverse = SCALE / z
+    col_lse = after + jnp.log(z)
+    scale_g1[...] = jnp.broadcast_to(shrink * inverse, (8, ROWS))
+    factors[...] = jnp.broadcast_to(SCALE * jnp.exp(largest_cols - col_lse), (8, ROWS))
+    for b in range(BLOCKS):
+        loss_r[pl.ds(b, 1)] = col_lse[:, b * BLK : (b + 1) * BLK] - diagonals[b]
+    largest = jnp.maximum(jnp.max(x, axis=1, keepdims=True), msg)
+    summed = jnp.exp(msg - largest) + jnp.sum(jnp.exp(x - largest), axis=1, keepdims=True)
+    w_last[...] = e * inverse + jnp.exp(x - (largest + jnp.log(summed) - LOG_SCALE))
     for c in range(CHUNKS):
         for src, slot in ((r_hbm, c), (q_hbm, CHUNKS + c)):
-            for copy in copies(src, slot, c):
-                copy.wait_send()
+            sent(copies(src, slot, c))
+    sent(messages)
 
 
 def finish(
-    g1, g2, h1, e_own, r_own, m_col, z_col, m_first, bias, last_msg, last_q, loss_q, diagonal,
+    g1, g2, h1, e_own, r_own, scale_g1, factors, w_last, last_q, loss_q, loss_r,
     loss_q_out, loss_r_out, q_out, r_out,
-    x_ref, gq, gr, sems,
+    gq, gr, sems,
 ):
-    for b in range(BLOCKS):
-        rows = rows_of(b)
-        x = dot_rows(r_own[rows], last_q[...]) * SCALE
-        x_ref[rows] = jnp.where(bias[rows] < 0.0, MASKED, x)
-    msg = last_msg[:1]
-    largest = jnp.maximum(jnp.max(x_ref[...], axis=0, keepdims=True), msg)
-    summed = jnp.exp(msg - largest) + jnp.sum(jnp.exp(x_ref[...] - largest), axis=0, keepdims=True)
-    row_lse = largest + jnp.log(summed)
-    loss_q_out[...] = loss_q[...]
-    factors = []
-    copies = []
-    for b in range(BLOCKS):
-        rows = rows_of(b)
-        x = x_ref[rows]
-        before = m_col[rows]
-        after = jnp.maximum(before, jnp.max(x, axis=1, keepdims=True))
-        shrink = jnp.exp(before - after)
-        e = jnp.exp(x - after)
-        z = z_col[rows] * shrink + jnp.sum(e, axis=1, keepdims=True)
-        inverse = 1.0 / z
-        col_lse = to_lanes(after + jnp.log(z))
-        loss_r_out[pl.ds(b, 1)] = col_lse - diagonal[pl.ds(b, 1)]
-        factors.append(jnp.exp(m_first[:1, b * BLK : (b + 1) * BLK] - col_lse))
-        w = e * inverse + jnp.exp(x - row_lse)
-        total = g1[rows] * wide(shrink * inverse) + g2[rows] + dot(w.astype(BF16), last_q[...])
-        gr[rows] = (total * SCALE).astype(BF16)
-        copies.append(pltpu.make_async_copy(gr.at[rows], r_out.at[rows], sems.at[b]))
-        copies[-1].start()
-    factors = jnp.concatenate(factors, axis=1)
-    for b in range(BLOCKS):
-        rows = rows_of(b)
-        at_diagonal = lanes((BLK, ROWS)) == lax.broadcasted_iota(jnp.int32, (BLK, ROWS), 0) + b * BLK
-        w = e_own[rows] * factors - jnp.where(at_diagonal, 1.0, 0.0)
-        total = h1[rows] + dot(w.astype(BF16), r_own[...])
-        gq[rows] = (total * SCALE).astype(BF16)
-        copies.append(pltpu.make_async_copy(gq.at[rows], q_out.at[rows], sems.at[BLOCKS + b]))
-        copies[-1].start()
-    for copy in copies:
-        copy.wait()
+    writes = [
+        pltpu.make_async_copy(loss_q, loss_q_out, sems.at[0]),
+        pltpu.make_async_copy(loss_r, loss_r_out, sems.at[1]),
+    ]
+    for write in writes:
+        write.start()
+
+    def put(k, held, out, cols):
+        writes.append(pltpu.make_async_copy(held.at[:, cols], out.at[:, cols], sems.at[2 + k]))
+        writes[-1].start()
+
+    diagonal = jnp.where(eye(), SCALE, 0.0)
+    w_own = []
+    for b in range(BLOCKS):
+        at = slice(b * BLK, (b + 1) * BLK)
+        w = e_own[rows_of(b)] * factors[:1]
+        w_own.append(jnp.concatenate([p for p in (w[:, : at.start], w[:, at] - diagonal, w[:, at.stop :]) if p.shape[1]], axis=1))
+    w_own = jnp.concatenate(w_own, axis=0).astype(BF16)
+    for k in range(PARTS):
+        cols = pl.ds(k * WIDTH, WIDTH)
+        gq[:, cols] = (h1[:, cols] + dot(w_own, r_own[:, cols])).astype(BF16)
+        put(k, gq, q_out, cols)
+    blocks = [slice(b * BLK, (b + 1) * BLK) for b in range(BLOCKS)]
+    w_cols = jnp.concatenate([jnp.transpose(w_last[:, at]) for at in blocks], axis=0).astype(BF16)
+    scale = [jnp.transpose(jnp.broadcast_to(scale_g1[:1, at], (BLK, BLK))) for at in blocks]
+    scale = jnp.concatenate(scale, axis=0)[:, :1]
+    for k in range(PARTS):
+        cols = pl.ds(k * WIDTH, WIDTH)
+        total = g1[:, cols] * scale + g2[:, cols] + dot(w_cols, last_q[:, cols])
+        gr[:, cols] = total.astype(BF16)
+        put(PARTS + k, gr, r_out, cols)
+    for write in writes:
+        write.wait()
 
 
 def shards(queries, responses, block_cluster):
@@ -310,11 +353,9 @@
         ((ROWS, D), F32),
         ((ROWS, ROWS), F32),
         ((ROWS, D), BF16),
-        ((ROWS, BLK), F32),
-        ((ROWS, BLK), F32),
         ((8, ROWS), F32),
-        ((ROWS, BLK), F32),
-        ((8, BLK), F32),
+        ((8, ROWS), F32),
+        ((BLK, ROWS), F32),
         ((BLK, D), BF16),
         ((BLOCKS, BLK), F32),
         ((BLOCKS, BLK), F32),
@@ -326,7 +367,9 @@
         out_specs=[vmem] * len(passed),
         scratch_shapes=[
             pltpu.VMEM((ROWS, D), BF16),
-            pltpu.VMEM((2 * CHUNKS, BLK, D), BF16),
+            pltpu.VMEM((ROWS, BLK), F32),
+            pltpu.VMEM((ROWS, BLK), F32),
+            pltpu.VMEM((2 * CHUNKS - 1, BLK, D), BF16),
             pltpu.VMEM((ROWS, ROWS), F32),
             pltpu.VMEM((ROWS, ROWS), F32),
             pltpu.VMEM((CHUNKS, ROWS, BLK), F32),
@@ -355,12 +398,11 @@
             jax.ShapeDtypeStruct((ROWS, D), BF16),
         ],
         in_specs=[vmem] * len(passed),
-        out_specs=[vmem, vmem, hbm, hbm],
+        out_specs=[hbm] * 4,
         scratch_shapes=[
-            pltpu.VMEM((ROWS, BLK), F32),
             pltpu.VMEM((ROWS, D), BF16),
             pltpu.VMEM((ROWS, D), BF16),
-            pltpu.SemaphoreType.DMA((2 * BLOCKS,)),
+            pltpu.SemaphoreType.DMA((2 + 2 * PARTS,)),
         ],
         compiler_params=pltpu.CompilerParams(vmem_limit_bytes=32 * 2**20),
         name="finish",

time: 45.7 us -> 44.2 us (0.967)
  the two profiles are of different devices: /device:TPU:1 before, /device:TPU:481 now
where the time goes in v3:
time: 44.2 us; the launch traced here: 44 us
  Pallas kernels  43.4 us (98%)
  between operations  0.64 us (1%)
    pallas_call x1, Pallas kernels, shards(): pl.pallas_call(exchange, out_shape=[pltpu.VMEM(shape, dtype) for shape, d...  41.5 us
    pallas_call x1, Pallas kernels, shards(): pl.pallas_call(finish, out_shape=[jax.ShapeDtypeStruct((BLOCKS, BLK), F32...  1.93 us

profile of v3, /device:TPU:481, one launch (start us, length us, event | category | flops | bytes accessed | tf_op | source)
XLA Modules:
  0.0 44.0 jit_solution(8200591992550207738)
XLA Ops:
  0.6 41.5 %exchange.1 = (f32[512,1024]{1,0:T(8,128)S(1)}, f32[512,1024]{1,0:T(8,128)S(1)}, f32[512,1024]{1,0:T(8,128)S(1)}, f32[512,512]{1,0:T(8,128)S(1)}, bf16[512,1024]...) custom-call(bf16[512,1024]{1,0:T(8,128)(2,1)} %q_hbm.1, ...), custom_call_target="tpu_custom_call" | custom-call | tf_op jit(solution)/shard_map/exchange/pallas_call | solution.py:363
  42.1 1.9 %finish.1 = (f32[4,128]{1,0:T(4,128)}, f32[4,128]{1,0:T(4,128)}, bf16[512,1024]{1,0:T(8,128)(2,1)}, bf16[512,1024]{1,0:T(8,128)(2,1)}) custom-call(f32[512,1024]{1,0:T(8,128)S(1)} %get-tuple-element.19.g1, f32[512,1024]{1,0:T(8,128)S(1)} %get-tuple-element.20.g2, f32[512,1024]{1,0:T(8,128)S(1)} %get-tuple-element.21.h1, ...), custom_call_target="tpu_custom_call" | custom-call | tf_op jit(solution)/shard_map/finish/pallas_call | solution.py:392

commit v4 on v3

--- a/solution.py
+++ b/solution.py
@@ -16,6 +16,10 @@
 SCALE = 20.0
 LOG_SCALE = math.log(SCALE)
 PARTS = 2
+R_PARCELS = ((0, 2), (2, 2), (4, 2))
+Q_PARCELS = ((0, 2), (2, 1), (3, 1), (4, 1))
+PARCELS = len(R_PARCELS) + len(Q_PARCELS) + 2
+EARLY = 768
 WIDTH = D // PARTS
 MASKED = -1e30
 F32 = jnp.float32
@@ -53,7 +57,7 @@
 
 
 def exchange(
-    q_hbm, r_hbm, cluster_hbm,
+    q_hbm, r_hbm, q_parts, r_parts, cluster_hbm,
     g1, g2, h1, e_own, r_own, scale_g1, factors, w_last, last_q, loss_q, loss_r,
     q_own, m_col, z_col, held, s_own, t_own, x_ref, msg_right, msg_left, got_left, got_right, ids,
     send_sem, recv_sem, msg_send, msg_recv, load_sem,
@@ -85,25 +89,29 @@
         def _():
             pl.semaphore_wait(barrier, signals)
 
-    def copies(src, slot, c):
-        landing = last_q if isinstance(slot, int) and slot == 2 * CHUNKS - 1 else held.at[slot]
-        to_right = pltpu.make_async_remote_copy(
-            src_ref=src.at[pl.ds(BLK + c * HALF, HALF)],
-            dst_ref=landing.at[pl.ds(0, HALF)],
-            send_sem=send_sem.at[slot, 0],
-            recv_sem=recv_sem.at[slot, 0],
-            device_id=coords(right),
-            device_id_type=MESH,
-        )
-        to_left = pltpu.make_async_remote_copy(
-            src_ref=src.at[pl.ds(c * HALF, HALF)],
-            dst_ref=landing.at[pl.ds(HALF, HALF)],
-            send_sem=send_sem.at[slot, 1],
-            recv_sem=recv_sem.at[slot, 1],
-            device_id=coords(left),
-            device_id_type=MESH,
-        )
-        return to_right, to_left
+    early, late = pl.ds(0, EARLY), pl.ds(EARLY, D - EARLY)
+    last = CHUNKS - 1
+    parcels = [(r_parts, first, n, held.at[pl.ds(first, n)], None) for first, n in R_PARCELS]
+    parcels += [(q_parts, first, n, held.at[pl.ds(CHUNKS + first, n)], None) for first, n in Q_PARCELS]
+    parcels += [(q_parts, last, 1, last_q, cols) for cols in (early, late)]
+
+    def copies(k):
+        src, first, n, dst, cols = parcels[k]
+        pair = []
+        for side, p in enumerate((right, left)):
+            begin = first if side else first + BLK // HALF
+            half = pl.ds(side * HALF, HALF)
+            pair.append(
+                pltpu.make_async_remote_copy(
+                    src_ref=src.at[pl.ds(begin, n)] if cols is None else src.at[begin, :, cols],
+                    dst_ref=dst.at[:, half] if cols is None else dst.at[half, cols],
+                    send_sem=send_sem.at[k, side],
+                    recv_sem=recv_sem.at[k, side],
+                    device_id=coords(p),
+                    device_id_type=MESH,
+                )
+            )
+        return pair
 
     def started(pair):
         to_right, to_left = pair
@@ -120,17 +128,10 @@
         pl.when(has_right)(to_right.wait_send)
         pl.when(has_left)(to_left.wait_send)
 
-    def start(src, slot, c):
-        started(copies(src, slot, c))
-
-    def landed(src, slot, c):
-        received(copies(src, slot, c))
-
-    start(r_hbm, 0, 0)
+    for k in range(len(R_PARCELS)):
+        started(copies(k))
     for load in loads:
         load.start()
-    for c in range(1, CHUNKS):
-        start(r_hbm, c, c)
 
     for exists, at, got in ((has_left, 0, got_left), (has_right, HALF, got_right)):
 
@@ -182,8 +183,8 @@
         for k, (src, dst, p) in enumerate(((msg_right, got_left, right), (msg_left, got_right, left)))
     ]
     started(messages)
-    for c in range(CHUNKS):
-        start(q_hbm, CHUNKS + c, c)
+    for k in range(len(R_PARCELS), len(parcels)):
+        started(copies(k))
 
     for b in range(BLOCKS):
         rows = rows_of(b)
@@ -217,10 +218,10 @@
         shape = (BLK, ROWS)
         return lanes(shape) == lax.broadcasted_iota(jnp.int32, shape, 0) + b * BLK
 
-    @pl.loop(0, CHUNKS)
-    def _(c):
-        landed(r_hbm, c, c)
-        scores_of(c, held.at[c], q_own)
+    for k, (first, n) in enumerate(R_PARCELS):
+        received(copies(k))
+        for c in range(first, first + n):
+            scores_of(c, held.at[c], q_own)
 
     received(messages)
     col_lse = jnp.concatenate([lse_of(c, c) for c in range(CHUNKS)], axis=1)
@@ -250,10 +251,11 @@
 
     for first, end in ((0, CHUNKS // 2), (CHUNKS // 2, CHUNKS - 1)):
 
-        @pl.loop(first, end)
-        def _(c):
-            landed(q_hbm, CHUNKS + c, c)
-            scores_of(c, held.at[CHUNKS + c], r_own)
+        for k, (src, begin, n, _, cols) in enumerate(parcels):
+            if src is q_parts and cols is None and first <= begin < end:
+                received(copies(k))
+                for c in range(begin, begin + n):
+                    scores_of(c, held.at[CHUNKS + c], r_own)
 
         group = range(first, end)
         lse = jnp.concatenate([lse_of(c, 8 + c) for c in group], axis=1)
@@ -280,8 +282,11 @@
         lax.broadcasted_iota(jnp.int32, shape, 0) < HALF, ids[left * BLOCKS + 1 + c // 2], ids[right * BLOCKS + c // 2]
     )
     allowed = id_chunk == jnp.broadcast_to(id_row, shape)
-    landed(q_hbm, CHUNKS + c, c)
-    x = jnp.where(allowed, dot_rows(last_q[...], r_own[...]) * SCALE, MASKED)
+    received(copies(len(parcels) - 2))
+    x = dot_rows(last_q[:, early], r_own[:, early])
+    received(copies(len(parcels) - 1))
+    x += dot_rows(last_q[:, late], r_own[:, late])
+    x = jnp.where(allowed, x * SCALE, MASKED)
     after = jnp.maximum(before, jnp.max(x, axis=0, keepdims=True))
     shrink = jnp.exp(before - after)
     e = jnp.exp(x - after)
@@ -295,9 +300,8 @@
     largest = jnp.maximum(jnp.max(x, axis=1, keepdims=True), msg)
     summed = jnp.exp(msg - largest) + jnp.sum(jnp.exp(x - largest), axis=1, keepdims=True)
     w_last[...] = e * inverse + jnp.exp(x - (largest + jnp.log(summed) - LOG_SCALE))
-    for c in range(CHUNKS):
-        for src, slot in ((r_hbm, c), (q_hbm, CHUNKS + c)):
-            sent(copies(src, slot, c))
+    for k in range(len(parcels)):
+        sent(copies(k))
     sent(messages)
 
 
@@ -342,6 +346,9 @@
 
 
 def shards(queries, responses, block_cluster):
+    parts = [
+        pltpu.with_memory_space_constraint(a.reshape(ROWS // HALF, HALF, D), pltpu.HBM) for a in (queries, responses)
+    ]
     queries, responses, block_cluster = (
         pltpu.with_memory_space_constraint(a, pltpu.HBM) for a in (queries, responses, block_cluster)
     )
@@ -360,10 +367,10 @@
         ((BLOCKS, BLK), F32),
         ((BLOCKS, BLK), F32),
     )
-    parts = pl.pallas_call(
+    sums = pl.pallas_call(
         exchange,
         out_shape=[pltpu.VMEM(shape, dtype) for shape, dtype in passed],
-        in_specs=[hbm] * 3,
+        in_specs=[hbm] * 5,
         out_specs=[vmem] * len(passed),
         scratch_shapes=[
             pltpu.VMEM((ROWS, D), BF16),
@@ -378,8 +385,8 @@
             pltpu.VMEM((16, BLK), F32),
             pltpu.VMEM((16, BLK), F32),
             pltpu.SMEM(block_cluster.shape, jnp.int32),
-            pltpu.SemaphoreType.DMA((2 * CHUNKS, 2)),
-            pltpu.SemaphoreType.DMA((2 * CHUNKS, 2)),
+            pltpu.SemaphoreType.DMA((PARCELS, 2)),
+            pltpu.SemaphoreType.DMA((PARCELS, 2)),
             pltpu.SemaphoreType.DMA((2,)),
             pltpu.SemaphoreType.DMA((2,)),
             pltpu.SemaphoreType.DMA((3,)),
@@ -388,7 +395,7 @@
             collective_id=0, has_side_effects=True, vmem_limit_bytes=32 * 2**20
         ),
         name="exchange",
-    )(queries, responses, block_cluster)
+    )(queries, responses, *parts, block_cluster)
     query_loss, response_loss, query_grad, response_grad = pl.pallas_call(
         finish,
         out_shape=[
@@ -406,7 +413,7 @@
         ],
         compiler_params=pltpu.CompilerParams(vmem_limit_bytes=32 * 2**20),
         name="finish",
-    )(*parts)
+    )(*sums)
     return query_loss.reshape(ROWS), response_loss.reshape(ROWS), query_grad, response_grad
 
 

time: 44.2 us -> 44.1 us (level)
  no operation moved by 1% of the time
where the time goes in v4:
time: 44.1 us; the launch traced here: 43.9 us
  Pallas kernels  43.3 us (98%)
  between operations  0.64 us (1%)
    pallas_call x1, Pallas kernels, shards(): pl.pallas_call(exchange, out_shape=[pltpu.VMEM(shape, dtype) for shape, d...  41.4 us
    pallas_call x1, Pallas kernels, shards(): pl.pallas_call(finish, out_shape=[jax.ShapeDtypeStruct((BLOCKS, BLK), F32...  1.93 us

profile of v4, /device:TPU:481, one launch (start us, length us, event | category | flops | bytes accessed | tf_op | source)
XLA Modules:
  0.0 43.9 jit_solution(18170861437886682764)
XLA Ops:
  0.6 41.4 %exchange.1 = (f32[512,1024]{1,0:T(8,128)S(1)}, f32[512,1024]{1,0:T(8,128)S(1)}, f32[512,1024]{1,0:T(8,128)S(1)}, f32[512,512]{1,0:T(8,128)S(1)}, bf16[512,1024]...) custom-call(bf16[512,1024]{1,0:T(8,128)(2,1)} %q_hbm.1, ...), custom_call_target="tpu_custom_call" | custom-call | tf_op jit(solution)/shard_map/exchange/pallas_call | solution.py:370
  42.0 1.9 %finish.1 = (f32[4,128]{1,0:T(4,128)}, f32[4,128]{1,0:T(4,128)}, bf16[512,1024]{1,0:T(8,128)(2,1)}, bf16[512,1024]{1,0:T(8,128)(2,1)}) custom-call(f32[512,1024]{1,0:T(8,128)S(1)} %get-tuple-element.19.g1, f32[512,1024]{1,0:T(8,128)S(1)} %get-tuple-element.20.g2, f32[512,1024]{1,0:T(8,128)S(1)} %get-tuple-element.21.h1, ...), custom_call_target="tpu_custom_call" | custom-call | tf_op jit(solution)/shard_map/finish/pallas_call | solution.py:399

commit v5 on v3

--- a/solution.py
+++ b/solution.py
@@ -159,17 +159,27 @@
 
     largest_cols, summed_cols = sums_by_lane(s_own)
     largest_rows, summed_rows = sums_by_lane(t_own)
-    for k, lse in enumerate((largest_cols + jnp.log(summed_cols), largest_rows + jnp.log(summed_rows))):
-        lse = jnp.broadcast_to(lse, (8, ROWS))
-        ahead, behind = pltpu.roll(lse, ROWS - HALF, 1), pltpu.roll(lse, HALF, 1)
-        for c in range(CHUNKS):
-            at = (c // 2) * BLK
-            row = pl.ds(8 * k + c, 1)
-            msg_right[row] = (ahead if c % 2 else lse)[:1, BLK + at : 2 * BLK + at]
-            msg_left[row] = (lse if c % 2 else behind)[:1, at : BLK + at]
-        rest = pl.ds(8 * k + CHUNKS, 8 - CHUNKS)
-        msg_right[rest] = jnp.zeros((8 - CHUNKS, BLK), F32)
-        msg_left[rest] = jnp.zeros((8 - CHUNKS, BLK), F32)
+    first_half = lanes((1, BLK)) < HALF
+    of_cols, of_rows = largest_cols + jnp.log(summed_cols), largest_rows + jnp.log(summed_rows)
+
+    def shifted(lse, by):
+        return pltpu.roll(jnp.broadcast_to(lse, (8, ROWS)), by, 1)[:1]
+
+    ahead = [shifted(lse, ROWS - HALF) for lse in (of_cols, of_rows)]
+    behind = [shifted(lse, HALF) for lse in (of_cols, of_rows)]
+    for c in range(CHUNKS):
+        here = slice((c // 2) * BLK, (c // 2 + 1) * BLK)
+        after = slice(here.start + BLK, here.stop + BLK)
+        row = pl.ds(c, 1)
+        if c % 2:
+            msg_right[row] = jnp.where(first_half, ahead[0][:, after], of_rows[:, after])
+            msg_left[row] = jnp.where(first_half, ahead[1][:, here], of_cols[:, here])
+        else:
+            msg_right[row] = jnp.where(first_half, of_cols[:, after], behind[1][:, after])
+            msg_left[row] = jnp.where(first_half, of_rows[:, here], behind[0][:, here])
+    rest = pl.ds(CHUNKS, 8 - CHUNKS)
+    for msg in (msg_right, msg_left):
+        msg[rest] = jnp.zeros((8 - CHUNKS, BLK), F32)
     messages = [
         pltpu.make_async_remote_copy(
             src_ref=src,
@@ -195,7 +205,12 @@
         g1[rows] = dot(e.astype(BF16), q_own[...])
     e_own[...] = jnp.exp(s_own[...] - largest_cols)
 
-    first_half = lanes((1, BLK)) < HALF
+    def cols_message(c):
+        return jnp.where(first_half, got_left[pl.ds(c, 1)], got_right[pl.ds(c, 1)])
+
+    def rows_message(c):
+        swapped = jnp.where(first_half, got_right[pl.ds(c, 1)], got_left[pl.ds(c, 1)])
+        return pltpu.roll(jnp.broadcast_to(swapped, (8, BLK)), HALF, 1)[:1]
 
     def ids_of(c):
         return jnp.where(first_half, ids[left * BLOCKS + 1 + c // 2], ids[right * BLOCKS + c // 2])
@@ -206,9 +221,8 @@
             allowed = jnp.broadcast_to(id_chunk == own_ids[b], (BLK, BLK))
             x_ref[c, rows_of(b)] = jnp.where(allowed, dot_rows(own[rows_of(b)], chunk[...]) * SCALE, MASKED)
 
-    def lse_of(c, msg_row):
+    def lse_of(c, msg):
         x = x_ref[c]
-        msg = jnp.where(first_half, got_left[pl.ds(msg_row, 1)], got_right[pl.ds(msg_row, 1)])
         largest = jnp.maximum(jnp.max(x, axis=0, keepdims=True), msg)
         summed = jnp.exp(msg - largest) + jnp.sum(jnp.exp(x - largest), axis=0, keepdims=True)
         return largest + jnp.log(summed)
@@ -223,7 +237,7 @@
         scores_of(c, held.at[c], q_own)
 
     received(messages)
-    col_lse = jnp.concatenate([lse_of(c, c) for c in range(CHUNKS)], axis=1)
+    col_lse = jnp.concatenate([lse_of(c, cols_message(c)) for c in range(CHUNKS)], axis=1)
     row_lse, diagonals = [], []
     for b in range(BLOCKS):
         rows = rows_of(b)
@@ -256,7 +270,7 @@
             scores_of(c, held.at[CHUNKS + c], r_own)
 
         group = range(first, end)
-        lse = jnp.concatenate([lse_of(c, 8 + c) for c in group], axis=1)
+        lse = jnp.concatenate([lse_of(c, rows_message(c)) for c in group], axis=1)
         for b in range(BLOCKS):
             rows = rows_of(b)
             x = jnp.concatenate([x_ref[c, rows] for c in group], axis=1)
@@ -273,7 +287,7 @@
     c = CHUNKS - 1
     before = jnp.concatenate([to_lanes(m_col[rows_of(b)]) for b in range(BLOCKS)], axis=1)
     z_before = jnp.concatenate([to_lanes(z_col[rows_of(b)]) for b in range(BLOCKS)], axis=1)
-    msg = jnp.where(first_half, got_left[pl.ds(8 + c, 1)], got_right[pl.ds(8 + c, 1)])
+    msg = rows_message(c)
     msg = jnp.sum(jnp.where(eye(), msg, 0.0), axis=1, keepdims=True)
     shape = (BLK, ROWS)
     id_chunk = jnp.where(
@@ -373,10 +387,10 @@
             pltpu.VMEM((ROWS, ROWS), F32),
             pltpu.VMEM((ROWS, ROWS), F32),
             pltpu.VMEM((CHUNKS, ROWS, BLK), F32),
-            pltpu.VMEM((16, BLK), F32),
-            pltpu.VMEM((16, BLK), F32),
-            pltpu.VMEM((16, BLK), F32),
-            pltpu.VMEM((16, BLK), F32),
+            pltpu.VMEM((8, BLK), F32),
+            pltpu.VMEM((8, BLK), F32),
+            pltpu.VMEM((8, BLK), F32),
+            pltpu.VMEM((8, BLK), F32),
             pltpu.SMEM(block_cluster.shape, jnp.int32),
             pltpu.SemaphoreType.DMA((2 * CHUNKS, 2)),
             pltpu.SemaphoreType.DMA((2 * CHUNKS, 2)),

time: 44.2 us -> 44.1 us (level)
  no operation moved by 1% of the time
where the time goes in v5:
time: 44.1 us; the launch traced here: 44 us
  Pallas kernels  43.3 us (98%)
  between operations  0.64 us (1%)
    pallas_call x1, Pallas kernels, shards(): pl.pallas_call(exchange, out_shape=[pltpu.VMEM(shape, dtype) for shape, d...  41.4 us
    pallas_call x1, Pallas kernels, shards(): pl.pallas_call(finish, out_shape=[jax.ShapeDtypeStruct((BLOCKS, BLK), F32...  1.93 us

profile of v5, /device:TPU:481, one launch (start us, length us, event | category | flops | bytes accessed | tf_op | source)
XLA Modules:
  0.0 44.0 jit_solution(12269706822915136307)
XLA Ops:
  0.6 41.4 %exchange.1 = (f32[512,1024]{1,0:T(8,128)S(1)}, f32[512,1024]{1,0:T(8,128)S(1)}, f32[512,1024]{1,0:T(8,128)S(1)}, f32[512,512]{1,0:T(8,128)S(1)}, bf16[512,1024]...) custom-call(bf16[512,1024]{1,0:T(8,128)(2,1)} %q_hbm.1, ...), custom_call_target="tpu_custom_call" | custom-call | tf_op jit(solution)/shard_map/exchange/pallas_call | solution.py:377
  42.0 1.9 %finish.1 = (f32[4,128]{1,0:T(4,128)}, f32[4,128]{1,0:T(4,128)}, bf16[512,1024]{1,0:T(8,128)(2,1)}, bf16[512,1024]{1,0:T(8,128)(2,1)}) custom-call(f32[512,1024]{1,0:T(8,128)S(1)} %get-tuple-element.19.g1, f32[512,1024]{1,0:T(8,128)S(1)} %get-tuple-element.20.g2, f32[512,1024]{1,0:T(8,128)S(1)} %get-tuple-element.21.h1, ...), custom_call_target="tpu_custom_call" | custom-call | tf_op jit(solution)/shard_map/finish/pallas_call | solution.py:406
